TPU v7x, 512 devices: a whole 4x8x8 slice. The times are simulated.
512 devices in a mesh: fsdp: 32 (over z_lo, x, core), tp: 16 (over z_hi, y).
Axes of the slice: x: 4, y: 8, z: 8 (z_hi: 2, z_lo: 4; z = z_hi * 4 + z_lo), core: 2. Of those that a mesh axis runs over, the one named last changes fastest.
Arguments:
- hidden: bfloat16 [4, 64, 5120], P(None, 'fsdp'), may hold values from -6 to 6
- base_kv: bfloat16 [5120, 2048], P(None, 'tp'), may hold values from -0.078125 to 0.078125
- delta_codes: bfloat16 [5120, 2048], P('fsdp', 'tp'), may hold values from -1 to 1
- block_scales: float32 [40, 16], P(None, 'tp'), may hold values from 0.004 to 0.04
- key_gain: float32 [128], replicated, may hold values from 2.5 to 6
- queries: bfloat16 [4, 64, 8192], P(None, 'fsdp', 'tp'), may hold values from -160 to 160
- kv_cache: bfloat16 [64, 4096, 2048], P('fsdp', None, 'tp'), may hold values from -6 to 6
- lengths: int32 [64], P('fsdp'), may hold values from 2 to 4096, as said below
Outputs:
- new_entries: bfloat16 [4, 64, 2048], P(None, 'fsdp', 'tp')
- attended: bfloat16 [4, 64, 8192], P(None, 'fsdp', 'tp')
Inputs may be any that keep to these rules, and one draw needn't show every extreme that they name: `lengths`: some row has exactly 4096 valid positions and some row exactly 2.
All inputs are finite; a program needn't handle non-finite values.
Results may differ from a plain program's by a relative error of at most 0.007.
Values may be sent and summed in bfloat16 or wider, within the bound.
A program may use at most 64 MiB of HBM per device.

v0:
```python
import math

import jax
import jax.numpy as jnp
from jax import lax
from jax.sharding import PartitionSpec as P

QH = 64
KVH = 8
HD = 128
BLOCK = 128


EPSILON = 1e-06
NEGATIVE = -1e30


def partner(block, axis, distance):
    count = lax.axis_size(axis)
    route = []
    for low in range(count):
        high = low | 1 << distance
        if high != low and high < count:
            route += [(low, high), (high, low)]
    return lax.ppermute(block, axis, route)


def attend(cache_full, fresh_full, fresh_allowed, in_cache, cache_values, fresh_values):
    factor = 1.0 / math.sqrt(HD)
    cache_logits = jnp.where(in_cache[None, :, None, None, :], cache_full * factor, NEGATIVE)
    fresh_logits = jnp.where(fresh_allowed[:, None, None, None, :], fresh_full * factor, NEGATIVE)
    highest = jnp.maximum(jnp.max(cache_logits, axis=-1), jnp.max(fresh_logits, axis=-1))
    cache_exp = jnp.exp(cache_logits - highest[..., None])
    fresh_exp = jnp.exp(fresh_logits - highest[..., None])
    denominator = jnp.sum(cache_exp, axis=-1) + jnp.sum(fresh_exp, axis=-1)
    cache_weights = (cache_exp / denominator[..., None]).astype(jnp.bfloat16)
    fresh_weights = (fresh_exp / denominator[..., None]).astype(jnp.bfloat16)
    combined = jnp.einsum(
        "srugl,rlud->srugd", cache_weights, cache_values, preferred_element_type=jnp.float32
    )
    combined = combined + jnp.einsum(
        "srugt,trud->srugd", fresh_weights, fresh_values, preferred_element_type=jnp.float32
    )
    return combined.astype(jnp.bfloat16)


def local(hidden, base_kv, delta_codes, block_scales, key_gain, queries, kv_cache, lengths):
    step_count, row_count, model_width = hidden.shape
    local_width = base_kv.shape[1]
    unit_count = local_width // HD
    half_dim = HD // 2
    group_size = QH // KVH
    cache_length = kv_cache.shape[1]
    partner_bit = lax.axis_size("tp").bit_length() - 2
    flattened = hidden.reshape(step_count * row_count, model_width)
    projected = jnp.dot(flattened, base_kv, preferred_element_type=jnp.float32)
    scale_full = jnp.repeat(jnp.repeat(block_scales, BLOCK, axis=0), BLOCK, axis=1)
    widened = flattened.astype(jnp.float32)
    correction = jnp.dot(
        widened,
        lax.all_gather(delta_codes, "fsdp", axis=0, tiled=True).astype(jnp.float32) * scale_full,
        precision=lax.Precision.HIGHEST,
    )
    projected = (projected + correction).reshape(step_count, row_count, unit_count, 2, half_dim)
    key_part = projected[:, :, :, 0, :]
    value_part = projected[:, :, :, 1, :]
    squares = jnp.sum(key_part * key_part, axis=-1)
    squares = squares + partner(squares, "tp", partner_bit)
    half_index = (lax.axis_index("tp") * unit_count + jnp.arange(unit_count)) // KVH
    gain_pairs = key_gain.reshape(2, half_dim)
    gain_units = jnp.where(half_index[:, None] == 0, gain_pairs[0][None, :], gain_pairs[1][None, :])
    normed = key_part * lax.rsqrt(squares / HD + EPSILON)[..., None] * gain_units
    entries = jnp.stack([normed, value_part], axis=3).astype(jnp.bfloat16)
    new_entries = entries.reshape(step_count, row_count, local_width)
    fresh_keys = entries[:, :, :, 0, :]
    fresh_values = entries[:, :, :, 1, :]
    query_units = queries.reshape(step_count, row_count, unit_count, group_size, half_dim)
    cache_units = kv_cache.reshape(row_count, cache_length, unit_count, 2, half_dim)
    cache_keys = cache_units[:, :, :, 0, :]
    cache_values = cache_units[:, :, :, 1, :]
    in_cache = jnp.arange(cache_length)[None, :] < lengths[:, None]
    steps_index = jnp.arange(step_count)
    fresh_allowed = steps_index[None, :] <= steps_index[:, None]
    outputs = []
    for current in range(step_count):
        query_step = query_units[current : current + 1]
        cache_full = jnp.einsum(
            "srugd,rlud->srugl", query_step, cache_keys, preferred_element_type=jnp.float32
        )
        fresh_full = jnp.einsum(
            "srugd,trud->srugt", query_step, fresh_keys, preferred_element_type=jnp.float32
        )
        other_cache, other_fresh = partner((cache_full, fresh_full), "tp", partner_bit)
        cache_full = cache_full + other_cache
        fresh_full = fresh_full + other_fresh
        outputs.append(
            attend(
                cache_full,
                fresh_full,
                fresh_allowed[current : current + 1],
                in_cache,
                cache_values,
                fresh_values,
            )
        )
    attended = jnp.concatenate(outputs, axis=0)
    attended = attended.reshape(step_count, row_count, unit_count * group_size * half_dim)
    return (new_entries, attended)


def solution(mesh):
    in_specs = (
        P(None, "fsdp", None),
        P(None, "tp"),
        P("fsdp", "tp"),
        P(None, "tp"),
        P(),
        P(None, "fsdp", "tp"),
        P("fsdp", None, "tp"),
        P("fsdp"),
    )
    out_specs = (P(None, "fsdp", "tp"), P(None, "fsdp", "tp"))
    return jax.shard_map(local, mesh=mesh, in_specs=in_specs, out_specs=out_specs, check_vma=False)
```

profile of v0, /device:TPU:6, one launch (start us, length us, event | category | flops | bytes accessed | tf_op | source)
XLA Modules:
  0.0 163.5 jit_solution(2655397339652615482)
XLA Ops:
  8.7 2.9 %copy.15 = bf16[2,4096,128]{1,2,0:T(8,128)(2,1)S(1)} copy(bf16[2,4096,128]{2,1,0:T(8,128)(2,1)} %param.14) | data formatting | bytes 4194304 | tf_op args[6]
  11.7 1.0 convolution_bitcast_fusion.3
  12.6 11.0 %collective-permute-start.1 = (f32[1,2,1,8,4096]{4,3,1,0,2:T(8,128)}, f32[1,2,1,8,4096]{4,3,1,0,2:T(8,128)}, u32[]{:S(2)}, u32[]{:S(2)}) collective-permute-start(f32[1,2,1,8,4096]{4,3,1,0,2:T(8,128)} %convolution_bitcast_fusion.3), channel_id=1, source_target_pairs={{0,8},{8,0},{1,9},{9,1},{2,10},{10,2},{3,11},{11,3},{4,12},{12,4},... | collective-permute-start | bytes 786440 | tf_op jit(solution)/shard_map/ppermute | solution.py:25
  23.8 1.0 convolution_bitcast_fusion.2
  24.7 1.9 %collective-permute-start.3 = (f32[1,2,1,8,4096]{4,3,1,0,2:T(8,128)}, f32[1,2,1,8,4096]{4,3,1,0,2:T(8,128)}, u32[]{:S(2)}, u32[]{:S(2)}) collective-permute-start(f32[1,2,1,8,4096]{4,3,1,0,2:T(8,128)} %convolution_bitcast_fusion.2), channel_id=1, source_target_pairs={{0,8},{8,0},{1,9},{9,1},{2,10},{10,2},{3,11},{11,3},{4,12},{12,4},... | collective-permute-start | bytes 786440 | tf_op jit(solution)/shard_map/ppermute | solution.py:25
  26.7 1.0 convolution_bitcast_fusion.1
  27.7 7.8 %collective-permute-start.5 = (f32[1,2,1,8,4096]{4,3,1,0,2:T(8,128)}, f32[1,2,1,8,4096]{4,3,1,0,2:T(8,128)}, u32[]{:S(2)}, u32[]{:S(2)}) collective-permute-start(f32[1,2,1,8,4096]{4,3,1,0,2:T(8,128)} %convolution_bitcast_fusion.1), channel_id=1, source_target_pairs={{0,8},{8,0},{1,9},{9,1},{2,10},{10,2},{3,11},{11,3},{4,12},{12,4},... | collective-permute-start | bytes 786440 | tf_op jit(solution)/shard_map/ppermute | solution.py:25
  35.6 1.0 convolution_bitcast_fusion
  36.6 1.9 %collective-permute-start.7 = (f32[1,2,1,8,4096]{4,3,1,0,2:T(8,128)}, f32[1,2,1,8,4096]{4,3,1,0,2:T(8,128)}, u32[]{:S(2)}, u32[]{:S(2)}) collective-permute-start(f32[1,2,1,8,4096]{4,3,1,0,2:T(8,128)} %convolution_bitcast_fusion), channel_id=1, source_target_pairs={{0,8},{8,0},{1,9},{9,1},{2,10},{10,2},{3,11},{11,3},{4,12},{12,4},... | collective-permute-start | bytes 786440 | tf_op jit(solution)/shard_map/ppermute | solution.py:25
  40.0 0.9 reshape.378
  41.2 10.9 %collective-permute-done.3 = f32[1,2,1,8,4096]{4,3,1,0,2:T(8,128)} collective-permute-done((f32[1,2,1,8,4096]{4,3,1,0,2:T(8,128)}, f32[1,2,1,8,4096]{4,3,1,0,2:T(8,128)}, u32[]{:S(2)}, u32[]{:S(2)}) %collective-permute-start.3) | collective-permute-done | bytes 262176 | tf_op jit(solution)/shard_map/ppermute | solution.py:25
  52.0 18.0 %collective-permute-done.5 = f32[1,2,1,8,4096]{4,3,1,0,2:T(8,128)} collective-permute-done((f32[1,2,1,8,4096]{4,3,1,0,2:T(8,128)}, f32[1,2,1,8,4096]{4,3,1,0,2:T(8,128)}, u32[]{:S(2)}, u32[]{:S(2)}) %collective-permute-start.5) | collective-permute-done | bytes 262176 | tf_op jit(solution)/shard_map/ppermute | solution.py:25
  70.0 4.2 %collective-permute-done.7 = f32[1,2,1,8,4096]{4,3,1,0,2:T(8,128)} collective-permute-done((f32[1,2,1,8,4096]{4,3,1,0,2:T(8,128)}, f32[1,2,1,8,4096]{4,3,1,0,2:T(8,128)}, u32[]{:S(2)}, u32[]{:S(2)}) %collective-permute-start.7) | collective-permute-done | bytes 262176 | tf_op jit(solution)/shard_map/ppermute | solution.py:25
  74.2 3.2 %fusion.43 = (f32[2,8]{1,0:T(2,128)}, f32[1,2,1,8,4096]{4,3,1,0,2:T(8,128)}, f32[2,8]{1,0:T(2,128)}, f32[1,2,1,8,4096]{4,3,1,0,2:T(8,128)}, f32[2,8]{1,0:T(2,128...) fusion(f32[1,2,1,8,4096]{4,3,1,0,2:T(8,128)} %convolution_bitcast_fusion.3, ...), kind=kLoop, calls=%fused_computation.96 | loop fusion | flops 1048512 | bytes 3154176 | tf_op jit(solution)/shard_map/reduce_max | solution.py:32
  77.3 35.6 %all-gather.2.cloned.1.call-done = bf16[5120,128]{1,0:T(8,128)(2,1)} async-done(((bf16[160,128]{1,0:T(8,128)(2,1)}), bf16[5120,128]{1,0:T(8,128)(2,1)}) %all-gather.2.cloned.1.call-update) | async-done | bytes 1310736 | tf_op jit(solution)/shard_map/all_gather | solution.py:61
  112.9 3.8 %fusion.11 = f32[8,128]{1,0:T(8,128)S(1)} fusion(f32[8,128]{1,0:T(8,128)S(1)} %fusion.51, bf16[8,5120]{1,0:T(8,128)(2,1)S(1)} %reshape.378, bf16[5120,128]{1,0:T(8,128)(2,1)} %all-gather.2.cloned.1.call-done, f32[5120]{0:T(1024)S(1)} %broadcast_bitcast_fusion), kind=kOutput, calls=%fused_computation.21 | convolution fusion | flops 64226304 | bytes 1421312 | tf_op jit(solution)/shard_map/dot_general | solution.py:59
  116.9 2.6 %collective-permute-start = (f32[4,2,1]{0,1,2:T(2,128)S(1)}, f32[4,2,1]{0,1,2:T(2,128)S(1)}, u32[]{:S(2)}, u32[]{:S(2)}) collective-permute-start(f32[4,2,1]{0,1,2:T(2,128)S(1)} %bitcast.155), channel_id=1, source_target_pairs={{0,8},{8,0},{1,9},{9,1},{2,10},{10,2},{3,11},{11,3},{4,12},{12,4},... | collective-permute-start | bytes 104 | tf_op jit(solution)/shard_map/ppermute | solution.py:25
  119.5 6.8 %collective-permute-done = f32[4,2,1]{0,1,2:T(2,128)S(1)} collective-permute-done((f32[4,2,1]{0,1,2:T(2,128)S(1)}, f32[4,2,1]{0,1,2:T(2,128)S(1)}, u32[]{:S(2)}, u32[]{:S(2)}) %collective-permute-start) | collective-permute-done | bytes 64 | tf_op jit(solution)/shard_map/ppermute | solution.py:25
  127.5 2.6 %collective-permute-start.2 = (f32[1,2,1,8,4]{3,4,1,0,2:T(4,128)S(1)}, f32[1,2,1,8,4]{3,4,1,0,2:T(4,128)S(1)}, u32[]{:S(2)}, u32[]{:S(2)}) collective-permute-start(f32[1,2,1,8,4]{3,4,1,0,2:T(4,128)S(1)} %convolution_bitcast_fusion.11), channel_id=1, source_target_pairs={{0,8},{8,0},{1,9},{9,1},{2,10},{10,2},{3,11},{11,3},{4,12},{12,4},... | collective-permute-start | bytes 776 | tf_op jit(solution)/shard_map/ppermute | solution.py:25
  130.1 7.2 %collective-permute-start.4 = (f32[1,2,1,8,4]{3,4,1,0,2:T(4,128)S(1)}, f32[1,2,1,8,4]{3,4,1,0,2:T(4,128)S(1)}, u32[]{:S(2)}, u32[]{:S(2)}) collective-permute-start(f32[1,2,1,8,4]{3,4,1,0,2:T(4,128)S(1)} %convolution_bitcast_fusion.10), channel_id=1, source_target_pairs={{0,8},{8,0},{1,9},{9,1},{2,10},{10,2},{3,11},{11,3},{4,12},{12,4},... | collective-permute-start | bytes 776 | tf_op jit(solution)/shard_map/ppermute | solution.py:25
  137.3 2.6 %collective-permute-start.6 = (f32[1,2,1,8,4]{3,4,1,0,2:T(4,128)S(1)}, f32[1,2,1,8,4]{3,4,1,0,2:T(4,128)S(1)}, u32[]{:S(2)}, u32[]{:S(2)}) collective-permute-start(f32[1,2,1,8,4]{3,4,1,0,2:T(4,128)S(1)} %convolution_bitcast_fusion.9), channel_id=1, source_target_pairs={{0,8},{8,0},{1,9},{9,1},{2,10},{10,2},{3,11},{11,3},{4,12},{12,4},... | collective-permute-start | bytes 776 | tf_op jit(solution)/shard_map/ppermute | solution.py:25
  139.9 7.2 %collective-permute-start.8 = (f32[1,2,1,8,4]{3,4,1,0,2:T(4,128)S(1)}, f32[1,2,1,8,4]{3,4,1,0,2:T(4,128)S(1)}, u32[]{:S(2)}, u32[]{:S(2)}) collective-permute-start(f32[1,2,1,8,4]{3,4,1,0,2:T(4,128)S(1)} %convolution_bitcast_fusion.8), channel_id=1, source_target_pairs={{0,8},{8,0},{1,9},{9,1},{2,10},{10,2},{3,11},{11,3},{4,12},{12,4},... | collective-permute-start | bytes 776 | tf_op jit(solution)/shard_map/ppermute | solution.py:25
  150.5 1.3 fusion.18
  151.8 1.4 convolution_bitcast_fusion.7
  (76 shorter events, 11.8 us)
Async XLA Ops:
  7.2 33.7 %copy-start = (bf16[5120,128]{1,0:T(8,128)(2,1)S(1)}, bf16[5120,128]{1,0:T(8,128)(2,1)}, u32[]{:S(2)}) copy-start(bf16[5120,128]{1,0:T(8,128)(2,1)} %param.9) | copy-start | bytes 3932164
  7.2 105.7 %all-gather.2.cloned.1.call-start = ((), (), s32[]{:S(2)}) async-start(), calls=%async_computation | async-start | bytes 1351680 | tf_op jit(solution)/shard_map/all_gather | solution.py:61
  12.6 26.5 %copy-start.8 = (f32[40,1]{0,1:T(1,128)S(1)}, f32[40,1]{0,1:T(1,128)}, u32[]{:S(2)}) copy-start(f32[40,1]{0,1:T(1,128)} %param.11) | copy-start | bytes 484
  12.6 26.6 %copy-start.7 = (s32[2]{0:T(128)S(1)}, s32[2]{0:T(128)}, u32[]{:S(2)}) copy-start(s32[2]{0:T(128)} %param.15) | copy-start | bytes 28
  12.6 26.7 %copy-start.6 = (f32[128]{0:T(128)S(1)}, f32[128]{0:T(128)}, u32[]{:S(2)}) copy-start(f32[128]{0:T(128)} %param.12) | copy-start | bytes 1540
  12.6 28.5 %collective-permute-start.1 = (f32[1,2,1,8,4096]{4,3,1,0,2:T(8,128)}, f32[1,2,1,8,4096]{4,3,1,0,2:T(8,128)}, u32[]{:S(2)}, u32[]{:S(2)}) collective-permute-start(f32[1,2,1,8,4096]{4,3,1,0,2:T(8,128)} %convolution_bitcast_fusion.3), channel_id=1, source_target_pairs={{0,8},{8,0},{1,9},{9,1},{2,10},{10,2},{3,11},{11,3},{4,12},{12,4},... | collective-permute-start | bytes 786440 | tf_op jit(solution)/shard_map/ppermute | solution.py:25
  24.7 27.3 %collective-permute-start.3 = (f32[1,2,1,8,4096]{4,3,1,0,2:T(8,128)}, f32[1,2,1,8,4096]{4,3,1,0,2:T(8,128)}, u32[]{:S(2)}, u32[]{:S(2)}) collective-permute-start(f32[1,2,1,8,4096]{4,3,1,0,2:T(8,128)} %convolution_bitcast_fusion.2), channel_id=1, source_target_pairs={{0,8},{8,0},{1,9},{9,1},{2,10},{10,2},{3,11},{11,3},{4,12},{12,4},... | collective-permute-start | bytes 786440 | tf_op jit(solution)/shard_map/ppermute | solution.py:25
  27.7 42.3 %collective-permute-start.5 = (f32[1,2,1,8,4096]{4,3,1,0,2:T(8,128)}, f32[1,2,1,8,4096]{4,3,1,0,2:T(8,128)}, u32[]{:S(2)}, u32[]{:S(2)}) collective-permute-start(f32[1,2,1,8,4096]{4,3,1,0,2:T(8,128)} %convolution_bitcast_fusion.1), channel_id=1, source_target_pairs={{0,8},{8,0},{1,9},{9,1},{2,10},{10,2},{3,11},{11,3},{4,12},{12,4},... | collective-permute-start | bytes 786440 | tf_op jit(solution)/shard_map/ppermute | solution.py:25
  36.6 37.6 %collective-permute-start.7 = (f32[1,2,1,8,4096]{4,3,1,0,2:T(8,128)}, f32[1,2,1,8,4096]{4,3,1,0,2:T(8,128)}, u32[]{:S(2)}, u32[]{:S(2)}) collective-permute-start(f32[1,2,1,8,4096]{4,3,1,0,2:T(8,128)} %convolution_bitcast_fusion), channel_id=1, source_target_pairs={{0,8},{8,0},{1,9},{9,1},{2,10},{10,2},{3,11},{11,3},{4,12},{12,4},... | collective-permute-start | bytes 786440 | tf_op jit(solution)/shard_map/ppermute | solution.py:25
  116.9 9.4 %collective-permute-start = (f32[4,2,1]{0,1,2:T(2,128)S(1)}, f32[4,2,1]{0,1,2:T(2,128)S(1)}, u32[]{:S(2)}, u32[]{:S(2)}) collective-permute-start(f32[4,2,1]{0,1,2:T(2,128)S(1)} %bitcast.155), channel_id=1, source_target_pairs={{0,8},{8,0},{1,9},{9,1},{2,10},{10,2},{3,11},{11,3},{4,12},{12,4},... | collective-permute-start | bytes 104 | tf_op jit(solution)/shard_map/ppermute | solution.py:25
  127.5 20.2 %collective-permute-start.2 = (f32[1,2,1,8,4]{3,4,1,0,2:T(4,128)S(1)}, f32[1,2,1,8,4]{3,4,1,0,2:T(4,128)S(1)}, u32[]{:S(2)}, u32[]{:S(2)}) collective-permute-start(f32[1,2,1,8,4]{3,4,1,0,2:T(4,128)S(1)} %convolution_bitcast_fusion.11), channel_id=1, source_target_pairs={{0,8},{8,0},{1,9},{9,1},{2,10},{10,2},{3,11},{11,3},{4,12},{12,4},... | collective-permute-start | bytes 776 | tf_op jit(solution)/shard_map/ppermute | solution.py:25
  130.1 19.1 %collective-permute-start.4 = (f32[1,2,1,8,4]{3,4,1,0,2:T(4,128)S(1)}, f32[1,2,1,8,4]{3,4,1,0,2:T(4,128)S(1)}, u32[]{:S(2)}, u32[]{:S(2)}) collective-permute-start(f32[1,2,1,8,4]{3,4,1,0,2:T(4,128)S(1)} %convolution_bitcast_fusion.10), channel_id=1, source_target_pairs={{0,8},{8,0},{1,9},{9,1},{2,10},{10,2},{3,11},{11,3},{4,12},{12,4},... | collective-permute-start | bytes 776 | tf_op jit(solution)/shard_map/ppermute | solution.py:25
  137.3 16.9 %collective-permute-start.6 = (f32[1,2,1,8,4]{3,4,1,0,2:T(4,128)S(1)}, f32[1,2,1,8,4]{3,4,1,0,2:T(4,128)S(1)}, u32[]{:S(2)}, u32[]{:S(2)}) collective-permute-start(f32[1,2,1,8,4]{3,4,1,0,2:T(4,128)S(1)} %convolution_bitcast_fusion.9), channel_id=1, source_target_pairs={{0,8},{8,0},{1,9},{9,1},{2,10},{10,2},{3,11},{11,3},{4,12},{12,4},... | collective-permute-start | bytes 776 | tf_op jit(solution)/shard_map/ppermute | solution.py:25
  139.9 14.4 %collective-permute-start.8 = (f32[1,2,1,8,4]{3,4,1,0,2:T(4,128)S(1)}, f32[1,2,1,8,4]{3,4,1,0,2:T(4,128)S(1)}, u32[]{:S(2)}, u32[]{:S(2)}) collective-permute-start(f32[1,2,1,8,4]{3,4,1,0,2:T(4,128)S(1)} %convolution_bitcast_fusion.8), channel_id=1, source_target_pairs={{0,8},{8,0},{1,9},{9,1},{2,10},{10,2},{3,11},{11,3},{4,12},{12,4},... | collective-permute-start | bytes 776 | tf_op jit(solution)/shard_map/ppermute | solution.py:25
  147.7 5.8 %copy-start.3 = (f32[1,2,1,8,4096]{4,3,1,0,2:T(8,128)S(1)}, f32[1,2,1,8,4096]{4,3,1,0,2:T(8,128)}, u32[]{:S(2)}) copy-start(f32[1,2,1,8,4096]{4,3,1,0,2:T(8,128)} %get-tuple-element.19) | copy-start | bytes 786436
  151.8 2.4 %copy-start.5 = (pred[4]{0:T(512)(128)(4,1)S(1)}, pred[4]{0:T(512)(128)(4,1)}, u32[]{:S(2)}) copy-start(pred[4]{0:T(512)(128)(4,1)} %get-tuple-element.30) | copy-start | bytes 16
  151.8 2.5 %copy-start.4 = (pred[4]{0:T(512)(128)(4,1)S(1)}, pred[4]{0:T(512)(128)(4,1)}, u32[]{:S(2)}) copy-start(pred[4]{0:T(512)(128)(4,1)} %get-tuple-element.29) | copy-start | bytes 16
  151.8 2.6 %copy-start.1 = (f32[1,2,1,8,4096]{4,3,1,0,2:T(8,128)S(1)}, f32[1,2,1,8,4096]{4,3,1,0,2:T(8,128)}, u32[]{:S(2)}) copy-start(f32[1,2,1,8,4096]{4,3,1,0,2:T(8,128)} %get-tuple-element.23) | copy-start | bytes 786436
  151.8 2.6 %copy-start.2 = (f32[1,2,1,8,4096]{4,3,1,0,2:T(8,128)S(1)}, f32[1,2,1,8,4096]{4,3,1,0,2:T(8,128)}, u32[]{:S(2)}) copy-start(f32[1,2,1,8,4096]{4,3,1,0,2:T(8,128)} %get-tuple-element.21) | copy-start | bytes 786436
Sparse Core Ops, SparseCore 0:
  10.2 102.6 all-gather.1
where the time goes:
time: 165 us; the launch traced here: 164 us
  waiting for transfers between devices  76 us (46%)
  starting transfers between devices  44.8 us (27%)
  between operations  14.3 us (9%)
  matrix products  12 us (7%)
  other arithmetic  9.39 us (6%)
  local copies, waits for them, and re-layouts  7.09 us (4%)
    ppermute x9, starting transfers between devices, partner(): return lax.ppermute(block, axis, route)  44.7 us
    ppermute x9, waiting for transfers between devices, partner(): return lax.ppermute(block, axis, route)  39.8 us
    all_gather x1, waiting for transfers between devices, local(): lax.all_gather(delta_codes, 'fsdp', axis=0, tiled=True).astype(jnp.float32)  35.6 us
    dot_general x4, matrix products, local(): jnp.einsum('srugd,rlud->srugl', query_step, cache_keys, preferred_element...  3.85 us
    dot_general x1, matrix products, local(): jnp.dot(widened, lax.all_gather(delta_codes, 'fsdp', axis=0, tiled=True)....  3.81 us
  transfers between devices with their start and end apart: 10, of which 5 were waited for; matrix products, arithmetic and copies ran while one was open for 13% of the time, Pallas kernels for 0%

commit v1 on v0

--- a/solution.py
+++ b/solution.py
@@ -1,8 +1,11 @@
+import functools
 import math
 
 import jax
 import jax.numpy as jnp
 from jax import lax
+from jax.experimental import pallas as pl
+from jax.experimental.pallas import tpu as pltpu
 from jax.sharding import PartitionSpec as P
 
 QH = 64
@@ -13,6 +16,351 @@
 
 EPSILON = 1e-06
 NEGATIVE = -1e30
+
+CACHE_MOST = 6.0
+NORM_LIMIT = 480.0
+LEVELS = 32760.0
+
+MESH = pl.DeviceIdType.MESH
+F32 = jnp.float32
+BF16 = jnp.bfloat16
+CHUNK = 1024
+
+
+def pair_kernel(
+    zs, xcs, ys,
+    hid, base, codes, scales, gain, qry, cache, lens,
+    ne_out, att_out, flag_out,
+    qv, hv, base_v, gain_v, cache_v, w_v, q32, qbf, qoth, h32, hs, hr, lown, snd, rcv, ysend, yrecv, p3,
+    fl, fy, fx,
+    loc_sem, cache_sem, main_s, main_r, qx_s, qx_r, ag_s, ag_r, p1_s, p1_r, p2_s, p2_r, p3_s, p3_r,
+    fy_s, fy_r, fx_s, fx_r,
+):
+    f = lax.axis_index("fsdp")
+    t = lax.axis_index("tp")
+    zl = f // xcs
+    xc = lax.rem(f, xcs)
+    zh = t // ys
+    y = lax.rem(t, ys)
+    rows = cache.shape[0]
+    steps = qry.shape[0]
+    group = 8
+    half = HD // 2
+    nq = steps * group
+    per_row = cache.shape[1] // CHUNK
+    nchunk = rows * per_row
+    factor = 1.0 / math.sqrt(HD)
+
+    partner = (f, (1 - zh) * ys + y)
+
+    def z_peer(k):
+        return (lax.rem(zl + k, zs) * xcs + xc, t)
+
+    def x_peer(k):
+        return (zl * xcs + lax.rem(xc + k, xcs), t)
+
+    def y_peer(k):
+        return (f, zh * ys + lax.rem(y + k, ys))
+
+    barrier = pltpu.get_barrier_semaphore()
+    everyone = (
+        [partner]
+        + [z_peer(k) for k in range(1, zs)]
+        + [x_peer(k) for k in range(1, xcs)]
+        + [y_peer(k) for k in range(1, ys)]
+    )
+    for device in everyone:
+        pl.semaphore_signal(barrier, inc=1, device_id=device, device_id_type=MESH)
+
+    get_q = pltpu.make_async_copy(qry, qv, loc_sem.at[0])
+    get_h = pltpu.make_async_copy(hid, hv, loc_sem.at[1])
+    get_w = pltpu.make_async_copy(codes, w_v.at[xc], loc_sem.at[2])
+    get_b = pltpu.make_async_copy(base, base_v, loc_sem.at[3])
+    get_g = pltpu.make_async_copy(gain, gain_v, loc_sem.at[4])
+    get_q.start()
+    get_c = []
+    for i in range(nchunk):
+        r, c = i // per_row, i % per_row
+        part = pl.ds(c * CHUNK, CHUNK)
+        get_c.append(pltpu.make_async_copy(cache.at[r, part], cache_v.at[r, part], cache_sem.at[i]))
+    get_c[0].start()
+    get_h.start()
+    for copy in get_c[1:]:
+        copy.start()
+    get_w.start()
+    get_b.start()
+    get_g.start()
+
+    get_q.wait()
+    lane512 = lax.broadcasted_iota(jnp.int32, (8, group * half), 1)
+    sub512 = lax.broadcasted_iota(jnp.int32, (8, group * half), 0)
+    own512 = (lane512 // half) == sub512
+    sub = lax.broadcasted_iota(jnp.int32, (8, HD), 0)
+    lane = lax.broadcasted_iota(jnp.int32, (8, HD), 1)
+    odd = (sub % 2) == 1
+    for s in range(steps):
+        both = qv[s].astype(F32)
+        for r in range(rows):
+            spread = jnp.broadcast_to(both[r : r + 1], (8, group * half))
+            spread = jnp.where(own512, spread, 0.0)
+            folded = spread[:, 0:HD]
+            for j in range(1, group * half // HD):
+                folded = folded + spread[:, j * HD : (j + 1) * HD]
+            folded = jnp.where(odd, pltpu.roll(folded, half, 1), folded)
+            q32[r, s * group : (s + 1) * group, :] = folded
+    norms = []
+    for r in range(rows):
+        qbf[r] = q32[r].astype(BF16)
+        norms.append(jnp.sum(jnp.abs(q32[r]), axis=1, keepdims=True))
+    widest = jnp.max(norms[0], axis=0, keepdims=True)
+    for r in range(1, rows):
+        widest = jnp.maximum(widest, jnp.max(norms[r], axis=0, keepdims=True))
+    fl[0] = jnp.broadcast_to(widest, (8, HD))
+    to_code = [LEVELS / (CACHE_MOST * jnp.maximum(n, 1e-30)) for n in norms]
+
+    def logits(i):
+        r, c = i // per_row, i % per_row
+        get_c[i].wait()
+        block = cache_v[r, c * CHUNK : (c + 1) * CHUNK, :]
+        raw = lax.dot_general(qbf[r], block, (((1,), (1,)), ((), ())), preferred_element_type=F32)
+        lown[i] = raw * factor
+        snd[i] = jnp.round(raw * to_code[r]).astype(jnp.int32).astype(jnp.int16)
+
+    logits(0)
+
+    get_h.wait()
+    for s in range(steps):
+        h32[s * rows : (s + 1) * rows, :] = hv[s].astype(F32)
+    blocks = h32.shape[1] // BLOCK
+    own_blocks = blocks // zs
+    for j in range(blocks // 2):
+        low = h32[:, 2 * j * BLOCK : (2 * j + 1) * BLOCK]
+        high = h32[:, (2 * j + 1) * BLOCK : (2 * j + 2) * BLOCK]
+        hs[(2 * j) // own_blocks, (2 * j % own_blocks) * 8 : (2 * j % own_blocks) * 8 + 16, :] = jnp.concatenate(
+            [low, high], axis=0
+        ).astype(BF16)
+
+    get_w.wait()
+    pl.semaphore_wait(barrier, len(everyone))
+
+    def remote(src, dst, send, recv, device):
+        copy = pltpu.make_async_remote_copy(
+            src_ref=src, dst_ref=dst, send_sem=send, recv_sem=recv, device_id=device, device_id_type=MESH
+        )
+        copy.start()
+        return copy
+
+    main = [remote(snd.at[0], rcv.at[0], main_s.at[0], main_r.at[0], partner)]
+    sent_q = remote(qbf, qoth, qx_s, qx_r, partner)
+    sent_h = [
+        remote(hs.at[lax.rem(zl + k, zs)], hr.at[k - 1], p1_s.at[k - 1], p1_r.at[k - 1], z_peer(k))
+        for k in range(1, zs)
+    ]
+    sent_w = [
+        remote(w_v.at[xc], w_v.at[xc], ag_s.at[k - 1], ag_r.at[k - 1], x_peer(k)) for k in range(1, xcs)
+    ]
+    sent_y = [
+        remote(fl.at[0], fy.at[k - 1], fy_s.at[k - 1], fy_r.at[k - 1], y_peer(k)) for k in range(1, ys)
+    ]
+    for i in range(1, nchunk):
+        logits(i)
+        main.append(remote(snd.at[i], rcv.at[i], main_s.at[i], main_r.at[i], partner))
+
+    get_b.wait()
+    get_g.wait()
+    projected = jnp.dot(h32[...].astype(BF16), base_v[...], preferred_element_type=F32)
+
+    for copy in sent_y:
+        copy.wait_recv()
+    widest = fl[0]
+    for k in range(ys - 1):
+        widest = jnp.maximum(widest, fy[k])
+    fl[1] = widest
+    sent_x = [
+        remote(fl.at[1], fx.at[k - 1], fx_s.at[k - 1], fx_r.at[k - 1], x_peer(k)) for k in range(1, xcs)
+    ]
+
+    for copy in sent_h:
+        copy.wait_recv()
+    for copy in sent_w:
+        copy.wait_recv()
+    mine = hs[zl].astype(F32)
+    theirs = [hr[k].astype(F32) for k in range(zs - 1)]
+    weights = w_v[...].reshape(own_blocks * BLOCK, HD)
+    total = None
+    for b in range(own_blocks):
+        stacked = jnp.concatenate([part[b * 8 : (b + 1) * 8] for part in [mine] + theirs], axis=0).astype(BF16)
+        term = jnp.dot(stacked, weights[b * BLOCK : (b + 1) * BLOCK], preferred_element_type=F32)
+        term = term * scales[zl * own_blocks + b, 0]
+        total = term if total is None else total + term
+    for copy in sent_x:
+        copy.wait_recv()
+    for k in range(xcs - 1):
+        widest = jnp.maximum(widest, fx[k])
+    for k in range(1, zs):
+        ysend[k - 1, 0:8, :] = total[k * 8 : (k + 1) * 8]
+        ysend[k - 1, 8:16, :] = widest
+    sent_p = [
+        remote(
+            ysend.at[k - 1], yrecv.at[k - 1], p2_s.at[k - 1], p2_r.at[k - 1], z_peer(zs - k)
+        )
+        for k in range(1, zs)
+    ]
+    correction = total[0:8]
+    for k in range(1, zs):
+        sent_p[k - 1].wait_recv()
+        correction = correction + yrecv[k - 1, 0:8, :]
+        widest = jnp.maximum(widest, yrecv[k - 1, 8:16, :])
+    projected = projected + correction
+    p3[0, 0:8, :] = projected
+    p3[0, 8:16, :] = widest
+    sent_k = remote(p3.at[0], p3.at[1], p3_s, p3_r, partner)
+
+    sent_q.wait_recv()
+    step_size = []
+    for r in range(rows):
+        n = jnp.sum(jnp.abs(qoth[r].astype(F32)), axis=1, keepdims=True)
+        step_size.append(n * (CACHE_MOST * factor / LEVELS))
+    top = [jnp.full((nq, 1), NEGATIVE, F32) for _ in range(rows)]
+    den = [jnp.zeros((nq, 1), F32) for _ in range(rows)]
+    acc = [jnp.zeros((nq, HD), F32) for _ in range(rows)]
+
+    def merge(r, values, block):
+        highest = jnp.maximum(top[r], jnp.max(values, axis=1, keepdims=True))
+        weight = jnp.exp(values - highest)
+        keep = jnp.exp(top[r] - highest)
+        den[r] = den[r] * keep + jnp.sum(weight, axis=1, keepdims=True)
+        acc[r] = acc[r] * keep + jnp.dot(weight.astype(BF16), block, preferred_element_type=F32)
+        top[r] = highest
+
+    def take(i):
+        r, c = i // per_row, i % per_row
+        main[i].wait_recv()
+        values = lown[i] + rcv[i].astype(jnp.int32).astype(F32) * step_size[r]
+        place = c * CHUNK + lax.broadcasted_iota(jnp.int32, (nq, CHUNK), 1)
+        values = jnp.where(place < lens[r], values, NEGATIVE)
+        merge(r, values, cache_v[r, c * CHUNK : (c + 1) * CHUNK, :])
+
+    late = nchunk - 2
+    for i in range(late):
+        take(i)
+
+    sent_k.wait_recv()
+    other = p3[1, 0:8, :]
+    flag_out[...] = jnp.maximum(widest, p3[1, 8:16, :])
+    is_key = lane < half
+    squares = jnp.sum(jnp.where(is_key, projected * projected, 0.0), axis=1, keepdims=True)
+    squares = squares + jnp.sum(jnp.where(is_key, other * other, 0.0), axis=1, keepdims=True)
+    inverse = lax.rsqrt(squares / HD + EPSILON)
+    gains = jnp.broadcast_to(gain_v[...], (8, HD))
+    swapped = pltpu.roll(gains, half, 1)
+    first = zh == 0
+    own_gain = jnp.where(first, gains, swapped)
+    other_gain = jnp.where(first, swapped, gains)
+    entries = jnp.where(is_key, projected * inverse * own_gain, projected)
+    other_keys = jnp.where(is_key, other * inverse * other_gain, 0.0)
+    for s in range(steps):
+        ne_out[s] = entries[s * rows : (s + 1) * rows, :].astype(BF16)
+    blank = jnp.zeros((8, HD), F32)
+    own16 = jnp.concatenate([entries, blank], axis=0).astype(BF16)
+    other16 = jnp.concatenate([other_keys, blank], axis=0).astype(BF16)
+    column = lax.broadcasted_iota(jnp.int32, (nq, 16), 1)
+    step_of = lax.broadcasted_iota(jnp.int32, (nq, 16), 0) // group
+    for r in range(rows):
+        fresh = lax.dot_general(qbf[r], own16, (((1,), (1,)), ((), ())), preferred_element_type=F32)
+        fresh = fresh + lax.dot_general(qoth[r], other16, (((1,), (1,)), ((), ())), preferred_element_type=F32)
+        allowed = (column % rows == r) & (column // rows <= step_of)
+        merge(r, jnp.where(allowed, fresh * factor, NEGATIVE), own16)
+
+    for i in range(late, nchunk):
+        take(i)
+
+    result = [acc[r] / den[r] for r in range(rows)]
+    right = (lane >= half) == odd
+    for s in range(steps):
+        lines = []
+        for r in range(rows):
+            part = result[r][s * group : (s + 1) * group, :]
+            part = jnp.where(odd, part, pltpu.roll(part, half, 1))
+            part = jnp.where(right, part, 0.0)
+            lines.append(
+                [
+                    jnp.sum(jnp.where(sub // 2 == j, part, 0.0), axis=0, keepdims=True)
+                    for j in range(group * half // HD)
+                ]
+            )
+        for j in range(group * half // HD):
+            att_out[s, :, j * HD : (j + 1) * HD] = jnp.concatenate([line[j] for line in lines], axis=0).astype(BF16)
+
+    for copy in main + [sent_q, sent_k] + sent_h + sent_w + sent_y + sent_x + sent_p:
+        copy.wait_send()
+
+
+def fused(sizes, hidden, base_kv, delta_codes, block_scales, key_gain, queries, kv_cache, lengths):
+    zs, xcs, ys = sizes
+    step_count, row_count, width = hidden.shape
+    cache_length = kv_cache.shape[1]
+    nq = step_count * 8
+    nchunk = row_count * cache_length // CHUNK
+    own_blocks = width // BLOCK // zs
+    dma = pltpu.SemaphoreType.DMA
+    any_space = pl.BlockSpec(memory_space=pl.ANY)
+    smem = pl.BlockSpec(memory_space=pltpu.SMEM)
+    vmem = pl.BlockSpec(memory_space=pltpu.VMEM)
+    return pl.pallas_call(
+        functools.partial(pair_kernel, zs, xcs, ys),
+        out_shape=(
+            jax.ShapeDtypeStruct((step_count, row_count, HD), BF16),
+            jax.ShapeDtypeStruct(queries.shape, BF16),
+            jax.ShapeDtypeStruct((8, HD), F32),
+        ),
+        in_specs=[any_space, any_space, any_space, smem, any_space, any_space, any_space, smem],
+        out_specs=(vmem, vmem, vmem),
+        scratch_shapes=[
+            pltpu.VMEM(queries.shape, BF16),
+            pltpu.VMEM(hidden.shape, BF16),
+            pltpu.VMEM(base_kv.shape, BF16),
+            pltpu.VMEM((1, HD), F32),
+            pltpu.VMEM(kv_cache.shape, BF16),
+            pltpu.VMEM((xcs,) + delta_codes.shape, BF16),
+            pltpu.VMEM((row_count, nq, HD), F32),
+            pltpu.VMEM((row_count, nq, HD), BF16),
+            pltpu.VMEM((row_count, nq, HD), BF16),
+            pltpu.VMEM((step_count * row_count, width), F32),
+            pltpu.VMEM((zs, own_blocks * 8, BLOCK), BF16),
+            pltpu.VMEM((zs - 1, own_blocks * 8, BLOCK), BF16),
+            pltpu.VMEM((nchunk, nq, CHUNK), F32),
+            pltpu.VMEM((nchunk, nq, CHUNK), jnp.int16),
+            pltpu.VMEM((nchunk, nq, CHUNK), jnp.int16),
+            pltpu.VMEM((zs - 1, 16, HD), F32),
+            pltpu.VMEM((zs - 1, 16, HD), F32),
+            pltpu.VMEM((2, 16, HD), F32),
+            pltpu.VMEM((2, 8, HD), F32),
+            pltpu.VMEM((ys - 1, 8, HD), F32),
+            pltpu.VMEM((xcs - 1, 8, HD), F32),
+            dma((5,)),
+            dma((nchunk,)),
+            dma((nchunk,)),
+            dma((nchunk,)),
+            dma,
+            dma,
+            dma((xcs - 1,)),
+            dma((xcs - 1,)),
+            dma((zs - 1,)),
+            dma((zs - 1,)),
+            dma((zs - 1,)),
+            dma((zs - 1,)),
+            dma,
+            dma,
+            dma((ys - 1,)),
+            dma((ys - 1,)),
+            dma((xcs - 1,)),
+            dma((xcs - 1,)),
+        ],
+        compiler_params=pltpu.CompilerParams(
+            collective_id=0, has_side_effects=True, vmem_limit_bytes=40 * 1024 * 1024
+        ),
+    )(hidden, base_kv, delta_codes, block_scales, key_gain.reshape(1, HD), queries, kv_cache, lengths)
 
 
 def partner(block, axis, distance):
@@ -44,7 +392,7 @@
     return combined.astype(jnp.bfloat16)
 
 
-def local(hidden, base_kv, delta_codes, block_scales, key_gain, queries, kv_cache, lengths):
+def plain(hidden, base_kv, delta_codes, block_scales, key_gain, queries, kv_cache, lengths):
     step_count, row_count, model_width = hidden.shape
     local_width = base_kv.shape[1]
     unit_count = local_width // HD
@@ -108,7 +456,20 @@
     return (new_entries, attended)
 
 
+def local(sizes, *args):
+    new_entries, attended, widest = fused(sizes, *args)
+    return lax.cond(
+        widest[0, 0] <= NORM_LIMIT,
+        lambda args, fast: fast,
+        lambda args, fast: plain(*args),
+        args,
+        (new_entries, attended),
+    )
+
+
 def solution(mesh):
+    fsdp, tp = mesh.shape["fsdp"], mesh.shape["tp"]
+    sizes = (4, fsdp // 4, tp // 2)
     in_specs = (
         P(None, "fsdp", None),
         P(None, "tp"),
@@ -120,4 +481,4 @@
         P("fsdp"),
     )
     out_specs = (P(None, "fsdp", "tp"), P(None, "fsdp", "tp"))
-    return jax.shard_map(local, mesh=mesh, in_specs=in_specs, out_specs=out_specs, check_vma=False)
+    return jax.shard_map(functools.partial(local, sizes), mesh=mesh, in_specs=in_specs, out_specs=out_specs, check_vma=False)

time: 165 us -> 206 us (1.25)
  Pallas kernels: 0 us -> 53.1 us
  waiting for transfers between devices: 76 us -> 65.6 us
  other arithmetic: 9.39 us -> 3.65 us
    pallas_call x0 -> x1, Pallas kernels: none -> 53.1 us  [fused(): pl.pallas_call(functools.partial(pair_kernel, zs, xcs, ys), out_shape=(ja...]
    ppermute x9, waiting for transfers between devices: 39.8 us -> 33 us  [partner(): return lax.ppermute(block, axis, route)]
    all_gather x1, waiting for transfers between devices: 35.6 us -> 31.9 us  [plain(): lax.all_gather(delta_codes, 'fsdp', axis=0, tiled=True).astype(jnp.float32)]
    another operation x4 -> x5, local copies, waits for them, and re-layouts: 0.34 us -> 3.25 us
  transfers between devices with their start and end apart: 10 -> 10, of which waited for: 5 -> 7; matrix products, arithmetic and copies ran while one was open for 13% -> 7% of each run, Pallas kernels for 0% -> 0%
where the time goes in v1:
time: 206 us; the launch traced here: 204 us
  waiting for transfers between devices  65.6 us (32%)
  Pallas kernels  53.1 us (26%)
  starting transfers between devices  45.8 us (22%)
  between operations  14.8 us (7%)
  matrix products  11.9 us (6%)
  local copies, waits for them, and re-layouts  8.73 us (4%)
  other arithmetic  3.65 us (2%)
    pallas_call x1, Pallas kernels, fused(): pl.pallas_call(functools.partial(pair_kernel, zs, xcs, ys), out_shape=(ja...  53.1 us
    ppermute x9, starting transfers between devices, partner(): return lax.ppermute(block, axis, route)  45.8 us
    ppermute x9, waiting for transfers between devices, partner(): return lax.ppermute(block, axis, route)  33 us
    all_gather x1, waiting for transfers between devices, plain(): lax.all_gather(delta_codes, 'fsdp', axis=0, tiled=True).astype(jnp.float32)  31.9 us
  transfers between devices with their start and end apart: 10, of which 7 were waited for; matrix products, arithmetic and copies ran while one was open for 7% of the time, Pallas kernels for 0%

profile of v1, /device:TPU:6, one launch (start us, length us, event | category | flops | bytes accessed | tf_op | source)
XLA Modules:
  0.0 203.8 jit_solution(12767553308946913798)
XLA Ops:
  8.1 53.1 %shard_map.99 = (bf16[4,2,128]{2,1,0:T(2,128)(2,1)}, bf16[4,2,512]{2,1,0:T(2,128)(2,1)S(1)}, f32[8,128]{1,0:T(8,128)S(1)}) custom-call(bf16[4,2,5120]{2,1,0:T(2,128)(2,1)} %hid.1, bf16[5120,128]{1,0:T(8,128)(2,1)} %base.1, bf16[160,128]{1,0:T(8,128)(2,1)} %codes.1, f32[40,1]{1,0:T(8,128)S(1)} %copy.22.scales, f32[1,128]{1,0:T(1,128)} %bitcast.157, ...), custom_call_target="tpu_custom_call" | custom-call | tf_op jit(solution)/shard_map/pallas_call | solution.py:310
  62.4 132.7 %conditional.1 = ((bf16[4,2,128]{2,1,0:T(2,128)(2,1)}, bf16[4,2,512]{2,1,0:T(2,128)(2,1)S(1)})) conditional(s32[]{:T(128)} %bitcast.61, (bf16[4,2,5120]{2,1,0:T(2,128)(2,1)S(1)}, bf16[5120,128]{1,0:T(8,128)(2,1)S(1)}, bf16[160,128]{1,0:T(8,128)(2,1)}, f32[40,1]{0,1:T(1,128)S(1)}, f32[128]{0:T(128)S(1)}, /*index=5*/s32[2]{0:T(128)S(1)}, ...), branch_computations={%region_0.18_spmd, %region_18.19_spmd} | conditional | flops 144280288 | bytes 30724384 | solution.py:461
  63.2 2.9 %copy.23 = bf16[2,4096,128]{1,2,0:T(8,128)(2,1)S(1)} copy(bf16[2,4096,128]{2,1,0:T(8,128)(2,1)} %get-tuple-element.46) | data formatting | bytes 4194304 | tf_op jit(solution)/shard_map
  66.2 1.0 convolution_bitcast_fusion.3
  67.1 2.0 collective-permute-start.1
  70.1 7.8 %collective-permute-start.3 = (f32[1,2,1,8,4096]{4,3,1,0,2:T(8,128)}, f32[1,2,1,8,4096]{4,3,1,0,2:T(8,128)}, u32[]{:S(2)}, u32[]{:S(2)}) collective-permute-start(f32[1,2,1,8,4096]{4,3,1,0,2:T(8,128)} %convolution_bitcast_fusion.2), channel_id=1, source_target_pairs={{0,8},{8,0},{1,9},{9,1},{2,10},{10,2},{3,11},{11,3},{4,12},{12,4},... | collective-permute-start | bytes 786440 | tf_op jit(solution)/shard_map/cond/branch_0_fun/ppermute | solution.py:373
  79.0 2.0 collective-permute-start.5
  81.0 1.0 convolution_bitcast_fusion
  82.0 7.8 %collective-permute-start.7 = (f32[1,2,1,8,4096]{4,3,1,0,2:T(8,128)}, f32[1,2,1,8,4096]{4,3,1,0,2:T(8,128)}, u32[]{:S(2)}, u32[]{:S(2)}) collective-permute-start(f32[1,2,1,8,4096]{4,3,1,0,2:T(8,128)} %convolution_bitcast_fusion), channel_id=1, source_target_pairs={{0,8},{8,0},{1,9},{9,1},{2,10},{10,2},{3,11},{11,3},{4,12},{12,4},... | collective-permute-start | bytes 786440 | tf_op jit(solution)/shard_map/cond/branch_0_fun/ppermute | solution.py:373
  91.8 1.2 fusion.51
  93.2 16.9 %collective-permute-done.3 = f32[1,2,1,8,4096]{4,3,1,0,2:T(8,128)} collective-permute-done((f32[1,2,1,8,4096]{4,3,1,0,2:T(8,128)}, f32[1,2,1,8,4096]{4,3,1,0,2:T(8,128)}, u32[]{:S(2)}, u32[]{:S(2)}) %collective-permute-start.3) | collective-permute-done | bytes 262176 | tf_op jit(solution)/shard_map/cond/branch_0_fun/ppermute | solution.py:373
  110.1 6.3 %collective-permute-done.5 = f32[1,2,1,8,4096]{4,3,1,0,2:T(8,128)} collective-permute-done((f32[1,2,1,8,4096]{4,3,1,0,2:T(8,128)}, f32[1,2,1,8,4096]{4,3,1,0,2:T(8,128)}, u32[]{:S(2)}, u32[]{:S(2)}) %collective-permute-start.5) | collective-permute-done | bytes 262176 | tf_op jit(solution)/shard_map/cond/branch_0_fun/ppermute | solution.py:373
  116.4 3.3 %collective-permute-done.7 = f32[1,2,1,8,4096]{4,3,1,0,2:T(8,128)} collective-permute-done((f32[1,2,1,8,4096]{4,3,1,0,2:T(8,128)}, f32[1,2,1,8,4096]{4,3,1,0,2:T(8,128)}, u32[]{:S(2)}, u32[]{:S(2)}) %collective-permute-start.7) | collective-permute-done | bytes 262176 | tf_op jit(solution)/shard_map/cond/branch_0_fun/ppermute | solution.py:373
  119.7 1.8 fusion.43
  121.5 31.9 %all-gather.2.cloned.1.call-done = bf16[5120,128]{1,0:T(8,128)(2,1)} async-done(((bf16[160,128]{1,0:T(8,128)(2,1)}), bf16[5120,128]{1,0:T(8,128)(2,1)}) %all-gather.2.cloned.1.call-update) | async-done | bytes 1310736 | tf_op jit(solution)/shard_map/cond/branch_0_fun/all_gather | solution.py:409
  153.3 3.8 %fusion.11 = f32[8,128]{1,0:T(8,128)S(1)} fusion(f32[8,128]{1,0:T(8,128)S(1)} %fusion.51, bf16[8,5120]{1,0:T(8,128)(2,1)S(1)} %copy-done.2, bf16[5120,128]{1,0:T(8,128)(2,1)} %all-gather.2.cloned.1.call-done, f32[5120]{0:T(1024)S(1)} %broadcast_bitcast_fusion), kind=kOutput, calls=%fused_computation.21 | convolution fusion | flops 64226304 | bytes 1421312 | tf_op jit(solution)/shard_map/cond/branch_0_fun/dot_general | solution.py:407
  157.4 6.8 %collective-permute-start = (f32[4,2,1]{0,1,2:T(2,128)S(1)}, f32[4,2,1]{0,1,2:T(2,128)S(1)}, u32[]{:S(2)}, u32[]{:S(2)}) collective-permute-start(f32[4,2,1]{0,1,2:T(2,128)S(1)} %bitcast.158), channel_id=1, source_target_pairs={{0,8},{8,0},{1,9},{9,1},{2,10},{10,2},{3,11},{11,3},{4,12},{12,4},... | collective-permute-start | bytes 104 | tf_op jit(solution)/shard_map/cond/branch_0_fun/ppermute | solution.py:373
  164.2 2.5 %collective-permute-done = f32[4,2,1]{0,1,2:T(2,128)S(1)} collective-permute-done((f32[4,2,1]{0,1,2:T(2,128)S(1)}, f32[4,2,1]{0,1,2:T(2,128)S(1)}, u32[]{:S(2)}, u32[]{:S(2)}) %collective-permute-start) | collective-permute-done | bytes 64 | tf_op jit(solution)/shard_map/cond/branch_0_fun/ppermute | solution.py:373
  167.3 6.8 %collective-permute-start.2 = (f32[1,2,1,8,4]{3,4,1,0,2:T(4,128)S(1)}, f32[1,2,1,8,4]{3,4,1,0,2:T(4,128)S(1)}, u32[]{:S(2)}, u32[]{:S(2)}) collective-permute-start(f32[1,2,1,8,4]{3,4,1,0,2:T(4,128)S(1)} %convolution_bitcast_fusion.11), channel_id=1, source_target_pairs={{0,8},{8,0},{1,9},{9,1},{2,10},{10,2},{3,11},{11,3},{4,12},{12,4},... | collective-permute-start | bytes 776 | tf_op jit(solution)/shard_map/cond/branch_0_fun/ppermute | solution.py:373
  174.2 2.9 %collective-permute-start.4 = (f32[1,2,1,8,4]{3,4,1,0,2:T(4,128)S(1)}, f32[1,2,1,8,4]{3,4,1,0,2:T(4,128)S(1)}, u32[]{:S(2)}, u32[]{:S(2)}) collective-permute-start(f32[1,2,1,8,4]{3,4,1,0,2:T(4,128)S(1)} %convolution_bitcast_fusion.10), channel_id=1, source_target_pairs={{0,8},{8,0},{1,9},{9,1},{2,10},{10,2},{3,11},{11,3},{4,12},{12,4},... | collective-permute-start | bytes 776 | tf_op jit(solution)/shard_map/cond/branch_0_fun/ppermute | solution.py:373
  177.1 6.8 %collective-permute-start.6 = (f32[1,2,1,8,4]{3,4,1,0,2:T(4,128)S(1)}, f32[1,2,1,8,4]{3,4,1,0,2:T(4,128)S(1)}, u32[]{:S(2)}, u32[]{:S(2)}) collective-permute-start(f32[1,2,1,8,4]{3,4,1,0,2:T(4,128)S(1)} %convolution_bitcast_fusion.9), channel_id=1, source_target_pairs={{0,8},{8,0},{1,9},{9,1},{2,10},{10,2},{3,11},{11,3},{4,12},{12,4},... | collective-permute-start | bytes 776 | tf_op jit(solution)/shard_map/cond/branch_0_fun/ppermute | solution.py:373
  183.9 2.9 %collective-permute-start.8 = (f32[1,2,1,8,4]{3,4,1,0,2:T(4,128)S(1)}, f32[1,2,1,8,4]{3,4,1,0,2:T(4,128)S(1)}, u32[]{:S(2)}, u32[]{:S(2)}) collective-permute-start(f32[1,2,1,8,4]{3,4,1,0,2:T(4,128)S(1)} %convolution_bitcast_fusion.8), channel_id=1, source_target_pairs={{0,8},{8,0},{1,9},{9,1},{2,10},{10,2},{3,11},{11,3},{4,12},{12,4},... | collective-permute-start | bytes 776 | tf_op jit(solution)/shard_map/cond/branch_0_fun/ppermute | solution.py:373
  189.5 3.9 %collective-permute-done.8 = f32[1,2,1,8,4]{3,4,1,0,2:T(4,128)S(1)} collective-permute-done((f32[1,2,1,8,4]{3,4,1,0,2:T(4,128)S(1)}, f32[1,2,1,8,4]{3,4,1,0,2:T(4,128)S(1)}, u32[]{:S(2)}, u32[]{:S(2)}) %collective-permute-start.8) | collective-permute-done | bytes 288 | tf_op jit(solution)/shard_map/cond/branch_0_fun/ppermute | solution.py:373
  195.1 1.3 copy.36
  (86 shorter events, 12.2 us)
Async XLA Ops:
  7.2 55.2 %copy-start.10 = (f32[40,1]{0,1:T(1,128)S(1)}, f32[40,1]{0,1:T(1,128)}, u32[]{:S(2)}) copy-start(f32[40,1]{0,1:T(1,128)} %param.13) | copy-start | bytes 484
  7.2 55.2 %copy-start.4 = (f32[128]{0:T(128)S(1)}, f32[128]{0:T(128)}, u32[]{:S(2)}) copy-start(f32[128]{0:T(128)} %param.14) | copy-start | bytes 1540
  7.2 55.2 %copy-start.1 = (bf16[4,2,5120]{2,1,0:T(2,128)(2,1)S(1)}, bf16[4,2,5120]{2,1,0:T(2,128)(2,1)}, u32[]{:S(2)}) copy-start(bf16[4,2,5120]{2,1,0:T(2,128)(2,1)} %hid.1) | copy-start | bytes 245764
  7.2 55.2 %copy-start = (bf16[5120,128]{1,0:T(8,128)(2,1)S(1)}, bf16[5120,128]{1,0:T(8,128)(2,1)}, u32[]{:S(2)}) copy-start(bf16[5120,128]{1,0:T(8,128)(2,1)} %base.1) | copy-start | bytes 3932164
  7.2 55.2 %copy-start.3 = (bf16[4,2,512]{2,1,0:T(2,128)(2,1)S(1)}, bf16[4,2,512]{2,1,0:T(2,128)(2,1)}, u32[]{:S(2)}) copy-start(bf16[4,2,512]{2,1,0:T(2,128)(2,1)} %qry.1) | copy-start | bytes 24580
  7.2 55.2 %copy-start.5 = (s32[2]{0:T(128)S(1)}, s32[2]{0:T(128)}, u32[]{:S(2)}) copy-start(s32[2]{0:T(128)} %lens.1) | copy-start | bytes 28
  62.4 90.9 %all-gather.2.cloned.1.call-start = ((), (), s32[]{:S(2)}) async-start(), calls=%async_computation | async-start | bytes 1351680 | tf_op jit(solution)/shard_map/cond/branch_0_fun/all_gather | solution.py:409
  67.1 26.1 %collective-permute-start.1 = (f32[1,2,1,8,4096]{4,3,1,0,2:T(8,128)}, f32[1,2,1,8,4096]{4,3,1,0,2:T(8,128)}, u32[]{:S(2)}, u32[]{:S(2)}) collective-permute-start(f32[1,2,1,8,4096]{4,3,1,0,2:T(8,128)} %convolution_bitcast_fusion.3), channel_id=1, source_target_pairs={{0,8},{8,0},{1,9},{9,1},{2,10},{10,2},{3,11},{11,3},{4,12},{12,4},... | collective-permute-start | bytes 786440 | tf_op jit(solution)/shard_map/cond/branch_0_fun/ppermute | solution.py:373
  70.1 40.0 %collective-permute-start.3 = (f32[1,2,1,8,4096]{4,3,1,0,2:T(8,128)}, f32[1,2,1,8,4096]{4,3,1,0,2:T(8,128)}, u32[]{:S(2)}, u32[]{:S(2)}) collective-permute-start(f32[1,2,1,8,4096]{4,3,1,0,2:T(8,128)} %convolution_bitcast_fusion.2), channel_id=1, source_target_pairs={{0,8},{8,0},{1,9},{9,1},{2,10},{10,2},{3,11},{11,3},{4,12},{12,4},... | collective-permute-start | bytes 786440 | tf_op jit(solution)/shard_map/cond/branch_0_fun/ppermute | solution.py:373
  79.0 37.4 %collective-permute-start.5 = (f32[1,2,1,8,4096]{4,3,1,0,2:T(8,128)}, f32[1,2,1,8,4096]{4,3,1,0,2:T(8,128)}, u32[]{:S(2)}, u32[]{:S(2)}) collective-permute-start(f32[1,2,1,8,4096]{4,3,1,0,2:T(8,128)} %convolution_bitcast_fusion.1), channel_id=1, source_target_pairs={{0,8},{8,0},{1,9},{9,1},{2,10},{10,2},{3,11},{11,3},{4,12},{12,4},... | collective-permute-start | bytes 786440 | tf_op jit(solution)/shard_map/cond/branch_0_fun/ppermute | solution.py:373
  82.0 37.7 %collective-permute-start.7 = (f32[1,2,1,8,4096]{4,3,1,0,2:T(8,128)}, f32[1,2,1,8,4096]{4,3,1,0,2:T(8,128)}, u32[]{:S(2)}, u32[]{:S(2)}) collective-permute-start(f32[1,2,1,8,4096]{4,3,1,0,2:T(8,128)} %convolution_bitcast_fusion), channel_id=1, source_target_pairs={{0,8},{8,0},{1,9},{9,1},{2,10},{10,2},{3,11},{11,3},{4,12},{12,4},... | collective-permute-start | bytes 786440 | tf_op jit(solution)/shard_map/cond/branch_0_fun/ppermute | solution.py:373
  91.7 61.6 %copy-start.2 = (bf16[8,5120]{1,0:T(8,128)(2,1)S(1)}, bf16[8,5120]{1,0:T(8,128)(2,1)}, u32[]{:S(2)}) copy-start(bf16[8,5120]{1,0:T(8,128)(2,1)} %reshape.364) | copy-start | bytes 245764 | tf_op jit(solution)/shard_map/cond
  93.0 73.7 %copy-start.9 = (f32[64]{0:T(128)S(1)}, f32[64]{0:T(128)}, u32[]{:S(2)}) copy-start(f32[64]{0:T(128)} %broadcast_select_fusion) | copy-start | bytes 772 | tf_op jit(solution)/shard_map/cond
  93.0 94.5 %copy-start.8 = (pred[4]{0:T(512)(128)(4,1)S(1)}, pred[4]{0:T(512)(128)(4,1)}, u32[]{:S(2)}) copy-start(pred[4]{0:T(512)(128)(4,1)} %get-tuple-element.74) | copy-start | bytes 16 | tf_op jit(solution)/shard_map/cond
  93.0 94.7 %copy-start.7 = (pred[4]{0:T(512)(128)(4,1)S(1)}, pred[4]{0:T(512)(128)(4,1)}, u32[]{:S(2)}) copy-start(pred[4]{0:T(512)(128)(4,1)} %get-tuple-element.77) | copy-start | bytes 16 | tf_op jit(solution)/shard_map/cond
  157.4 9.4 %collective-permute-start = (f32[4,2,1]{0,1,2:T(2,128)S(1)}, f32[4,2,1]{0,1,2:T(2,128)S(1)}, u32[]{:S(2)}, u32[]{:S(2)}) collective-permute-start(f32[4,2,1]{0,1,2:T(2,128)S(1)} %bitcast.158), channel_id=1, source_target_pairs={{0,8},{8,0},{1,9},{9,1},{2,10},{10,2},{3,11},{11,3},{4,12},{12,4},... | collective-permute-start | bytes 104 | tf_op jit(solution)/shard_map/cond/branch_0_fun/ppermute | solution.py:373
  167.3 20.2 %collective-permute-start.2 = (f32[1,2,1,8,4]{3,4,1,0,2:T(4,128)S(1)}, f32[1,2,1,8,4]{3,4,1,0,2:T(4,128)S(1)}, u32[]{:S(2)}, u32[]{:S(2)}) collective-permute-start(f32[1,2,1,8,4]{3,4,1,0,2:T(4,128)S(1)} %convolution_bitcast_fusion.11), channel_id=1, source_target_pairs={{0,8},{8,0},{1,9},{9,1},{2,10},{10,2},{3,11},{11,3},{4,12},{12,4},... | collective-permute-start | bytes 776 | tf_op jit(solution)/shard_map/cond/branch_0_fun/ppermute | solution.py:373
  174.2 13.5 %collective-permute-start.4 = (f32[1,2,1,8,4]{3,4,1,0,2:T(4,128)S(1)}, f32[1,2,1,8,4]{3,4,1,0,2:T(4,128)S(1)}, u32[]{:S(2)}, u32[]{:S(2)}) collective-permute-start(f32[1,2,1,8,4]{3,4,1,0,2:T(4,128)S(1)} %convolution_bitcast_fusion.10), channel_id=1, source_target_pairs={{0,8},{8,0},{1,9},{9,1},{2,10},{10,2},{3,11},{11,3},{4,12},{12,4},... | collective-permute-start | bytes 776 | tf_op jit(solution)/shard_map/cond/branch_0_fun/ppermute | solution.py:373
  177.1 12.3 %collective-permute-start.6 = (f32[1,2,1,8,4]{3,4,1,0,2:T(4,128)S(1)}, f32[1,2,1,8,4]{3,4,1,0,2:T(4,128)S(1)}, u32[]{:S(2)}, u32[]{:S(2)}) collective-permute-start(f32[1,2,1,8,4]{3,4,1,0,2:T(4,128)S(1)} %convolution_bitcast_fusion.9), channel_id=1, source_target_pairs={{0,8},{8,0},{1,9},{9,1},{2,10},{10,2},{3,11},{11,3},{4,12},{12,4},... | collective-permute-start | bytes 776 | tf_op jit(solution)/shard_map/cond/branch_0_fun/ppermute | solution.py:373
  183.9 9.4 %collective-permute-start.8 = (f32[1,2,1,8,4]{3,4,1,0,2:T(4,128)S(1)}, f32[1,2,1,8,4]{3,4,1,0,2:T(4,128)S(1)}, u32[]{:S(2)}, u32[]{:S(2)}) collective-permute-start(f32[1,2,1,8,4]{3,4,1,0,2:T(4,128)S(1)} %convolution_bitcast_fusion.8), channel_id=1, source_target_pairs={{0,8},{8,0},{1,9},{9,1},{2,10},{10,2},{3,11},{11,3},{4,12},{12,4},... | collective-permute-start | bytes 776 | tf_op jit(solution)/shard_map/cond/branch_0_fun/ppermute | solution.py:373
  188.0 1.3 copy-start.6
Sparse Core Ops, SparseCore 0:
  65.4 87.9 all-gather.1

commit v2 on v1

v2 whole, which is shorter than its diff:
```python
import functools
import math

import jax
import jax.numpy as jnp
from jax import lax
from jax.experimental import pallas as pl
from jax.experimental.pallas import tpu as pltpu
from jax.sharding import PartitionSpec as P

HD = 128
BLOCK = 128


EPSILON = 1e-06
NEGATIVE = -1e30

CACHE_MOST = 6.0
NORM_LIMIT = 480.0
LEVELS = 32760.0

MESH = pl.DeviceIdType.MESH
F32 = jnp.float32
BF16 = jnp.bfloat16
CHUNK = 1024
LATE = 8
FLAG_STEPS = {2: 2, 5: 3}


def pair_kernel(
    zs, xcs, ys, exact,
    hid, base, codes, scales, gain, qry, cache, lens,
    *refs,
):
    both_out, refs = refs[0], refs[1:]
    if not exact:
        flag_out, refs = refs[0], refs[1:]
    (
    qv, hv, base_v, gain_v, cache_v, w_v, q32, qbf, packed, qoth, h32, hs, hr, lown, snd, rcv, ysend, yrecv,
    fl, fy, fx, fz, fp,
    loc_sem, cache_sem, main_s, main_r, qx_s, qx_r, ag_s, ag_r, p1_s, p1_r, p2_s, p2_r,
    fy_s, fy_r, fx_s, fx_r, fz_s, fz_r, fp_s, fp_r,
    ) = refs
    f = lax.axis_index("fsdp")
    t = lax.axis_index("tp")
    zl = f // xcs
    xc = lax.rem(f, xcs)
    zh = t // ys
    y = lax.rem(t, ys)
    rows = cache.shape[0]
    steps = qry.shape[0]
    group = 8
    half = HD // 2
    nq = steps * group
    per_row = cache.shape[1] // CHUNK
    nchunk = rows * per_row
    factor = 1.0 / math.sqrt(HD)

    partner = (f, (1 - zh) * ys + y)

    def z_peer(k):
        return (lax.rem(zl + k, zs) * xcs + xc, t)

    def other_z_peer(k):
        return (lax.rem(zl + k, zs) * xcs + xc, (1 - zh) * ys + y)

    def x_peer(k):
        return (zl * xcs + lax.rem(xc + k, xcs), t)

    def y_peer(k):
        return (f, zh * ys + lax.rem(y + k, ys))

    barrier = pltpu.get_barrier_semaphore()
    everyone = (
        [partner]
        + [z_peer(k) for k in range(1, zs)]
        + [other_z_peer(k) for k in range(1, zs)]
        + [x_peer(k) for k in range(1, xcs)]
    )
    for device in everyone:
        pl.semaphore_signal(barrier, inc=1, device_id=device, device_id_type=MESH)

    first = zh == 0
    if not exact:

        @pl.when(first)
        def _():
            for k in range(1, ys):
                pl.semaphore_signal(barrier, inc=1, device_id=y_peer(k), device_id_type=MESH)

    get_q = pltpu.make_async_copy(qry, qv, loc_sem.at[0])
    get_h = pltpu.make_async_copy(hid, hv, loc_sem.at[1])
    get_w = pltpu.make_async_copy(codes, w_v.at[xc], loc_sem.at[2])
    get_b = pltpu.make_async_copy(base, base_v, loc_sem.at[3])
    get_g = pltpu.make_async_copy(gain, gain_v, loc_sem.at[4])
    get_q.start()
    get_c = []
    for i in range(nchunk):
        r, c = i // per_row, i % per_row
        part = pl.ds(c * CHUNK, CHUNK)
        get_c.append(pltpu.make_async_copy(cache.at[r, part], cache_v.at[r, part], cache_sem.at[i]))
    get_c[0].start()
    get_h.start()
    for copy in get_c[1:]:
        copy.start()
    get_w.start()
    get_b.start()
    get_g.start()

    get_q.wait()
    lane512 = lax.broadcasted_iota(jnp.int32, (8, group * half), 1)
    sub512 = lax.broadcasted_iota(jnp.int32, (8, group * half), 0)
    own512 = (lane512 // half) == sub512
    sub = lax.broadcasted_iota(jnp.int32, (8, HD), 0)
    lane = lax.broadcasted_iota(jnp.int32, (8, HD), 1)
    odd = (sub % 2) == 1
    for s in range(steps):
        both = qv[s].astype(F32)
        for r in range(rows):
            spread = jnp.broadcast_to(both[r : r + 1], (8, group * half))
            spread = jnp.where(own512, spread, 0.0)
            folded = spread[:, 0:HD]
            for j in range(1, group * half // HD):
                folded = folded + spread[:, j * HD : (j + 1) * HD]
            folded = jnp.where(odd, pltpu.roll(folded, half, 1), folded)
            q32[r, s * group : (s + 1) * group, :] = folded
    norms = []
    for r in range(rows):
        qbf[r] = q32[r].astype(BF16)
        norms.append(jnp.sum(jnp.abs(q32[r]), axis=1, keepdims=True))
    widest = jnp.max(norms[0], axis=0, keepdims=True)
    for r in range(1, rows):
        widest = jnp.maximum(widest, jnp.max(norms[r], axis=0, keepdims=True))
    wide_q = lax.broadcasted_iota(jnp.int32, (nq, HD), 1) < half
    packed[0] = (q32[0] + pltpu.roll(q32[1], half, 1)).astype(BF16)
    to_code = [LEVELS / (CACHE_MOST * jnp.maximum(n, 1e-30)) for n in norms]

    def logits(i):
        r, c = i // per_row, i % per_row
        get_c[i].wait()
        block = cache_v[r, c * CHUNK : (c + 1) * CHUNK, :]
        raw = lax.dot_general(qbf[r], block, (((1,), (1,)), ((), ())), preferred_element_type=F32)
        lown[i] = raw * factor
        if not exact:
            snd[i] = jnp.round(raw * to_code[r]).astype(jnp.int32).astype(jnp.int16)

    for i in range(nchunk):
        logits(i)

    get_h.wait()
    for s in range(steps):
        h32[s * rows : (s + 1) * rows, :] = hv[s].astype(F32)
    blocks = h32.shape[1] // BLOCK
    own_blocks = blocks // zs
    for j in range(blocks // 2):
        low = h32[:, 2 * j * BLOCK : (2 * j + 1) * BLOCK]
        high = h32[:, (2 * j + 1) * BLOCK : (2 * j + 2) * BLOCK]
        hs[(2 * j) // own_blocks, (2 * j % own_blocks) * 8 : (2 * j % own_blocks) * 8 + 16, :] = jnp.concatenate(
            [low, high], axis=0
        ).astype(BF16)

    get_w.wait()
    pl.semaphore_wait(barrier, len(everyone) + (0 if exact else (1 - zh) * (ys - 1)))

    def remote(src, dst, send, recv, device):
        copy = pltpu.make_async_remote_copy(
            src_ref=src, dst_ref=dst, send_sem=send, recv_sem=recv, device_id=device, device_id_type=MESH
        )
        copy.start()
        return copy

    sent_h = [
        remote(hs.at[lax.rem(zl + k, zs)], hr.at[k - 1], p1_s.at[k - 1], p1_r.at[k - 1], z_peer(k))
        for k in range(1, zs)
    ]
    sent_w = [
        remote(w_v.at[xc], w_v.at[xc], ag_s.at[k - 1], ag_r.at[k - 1], x_peer(k)) for k in range(1, xcs)
    ]
    sent_q = remote(packed.at[0], packed.at[1], qx_s, qx_r, partner)
    parts = lown if exact else snd
    main = [remote(parts.at[i], rcv.at[i], main_s.at[i], main_r.at[i], partner) for i in range(nchunk)]

    get_b.wait()
    get_g.wait()
    projected = jnp.dot(h32[...].astype(BF16), base_v[...], preferred_element_type=F32)

    sent_q.wait_recv()
    step_size = []
    lines = packed[1].astype(F32)
    for r in range(rows):
        line = jnp.where(wide_q, lines if r == 0 else pltpu.roll(lines, half, 1), 0.0)
        qoth[r] = line.astype(BF16)
        n = jnp.sum(jnp.abs(line), axis=1, keepdims=True)
        widest = jnp.maximum(widest, jnp.max(n, axis=0, keepdims=True))
        step_size.append(n * (CACHE_MOST * factor / LEVELS))

    def flag_copies(stage):
        src = fl.at[stage]
        if stage == 0:
            return [(src, fy.at[k - 1], fy_s.at[k - 1], fy_r.at[k - 1], y_peer(k)) for k in range(1, ys)]
        if stage == 1:
            return [(src, fx.at[k - 1], fx_s.at[k - 1], fx_r.at[k - 1], x_peer(k)) for k in range(1, xcs)]
        if stage == 2:
            return [(src, fz.at[k - 1], fz_s.at[k - 1], fz_r.at[k - 1], z_peer(k)) for k in range(1, zs)]
        return [(src, fp, fp_s, fp_r, partner)]

    def described(stage):
        return [
            pltpu.make_async_remote_copy(
                src_ref=src, dst_ref=dst, send_sem=send, recv_sem=recv, device_id=device, device_id_type=MESH
            )
            for src, dst, send, recv, device in flag_copies(stage)
        ]

    def flag_step(stage):
        if exact:
            return

        @pl.when(first)
        def _():
            if stage == 0:
                fl[0] = jnp.broadcast_to(widest, (8, HD))
            else:
                largest = fl[stage - 1]
                for copy, arrived in zip(described(stage - 1), flag_copies(stage - 1)):
                    copy.wait_recv()
                    largest = jnp.maximum(largest, arrived[1][...])
                fl[stage] = largest
            for copy in described(stage):
                copy.start()

    flag_step(0)

    for copy in sent_h:
        copy.wait_recv()
    for copy in sent_w:
        copy.wait_recv()
    mine = hs[zl].astype(F32)
    theirs = [hr[k].astype(F32) for k in range(zs - 1)]
    gathered = w_v[...]
    weights = gathered.reshape(own_blocks * BLOCK, HD)
    total = None
    for b in range(own_blocks):
        stacked = jnp.concatenate([part[b * 8 : (b + 1) * 8] for part in [mine] + theirs], axis=0).astype(BF16)
        term = jnp.dot(stacked, weights[b * BLOCK : (b + 1) * BLOCK], preferred_element_type=F32)
        term = term * scales[0, zl * own_blocks + b]
        total = term if total is None else total + term
    projected = projected + total[0:8]
    for k in range(1, zs):
        ysend[k] = total[k * 8 : (k + 1) * 8]
    ysend[0] = projected
    sent_p = [remote(ysend.at[0], yrecv.at[1, 0], p2_s.at[1, 0], p2_r.at[1, 0], partner)]
    for k in range(1, zs):
        for side, device in enumerate((z_peer(zs - k), other_z_peer(zs - k))):
            sent_p.append(remote(ysend.at[k], yrecv.at[side, k], p2_s.at[side, k], p2_r.at[side, k], device))

    flag_step(1)

    top = [jnp.full((nq, 1), NEGATIVE, F32) for _ in range(rows)]
    den = [jnp.zeros((nq, 1), F32) for _ in range(rows)]
    acc = [jnp.zeros((nq, HD), F32) for _ in range(rows)]

    def merge(r, values, block):
        highest = jnp.maximum(top[r], jnp.max(values, axis=1, keepdims=True))
        weight = jnp.exp(values - highest)
        keep = jnp.exp(top[r] - highest)
        den[r] = den[r] * keep + jnp.sum(weight, axis=1, keepdims=True)
        acc[r] = acc[r] * keep + jnp.dot(weight.astype(BF16), block, preferred_element_type=F32)
        top[r] = highest

    def take(i):
        r, c = i // per_row, i % per_row
        main[i].wait_recv()
        received = rcv[i] if exact else rcv[i].astype(jnp.int32).astype(F32) * step_size[r]
        values = lown[i] + received
        place = c * CHUNK + lax.broadcasted_iota(jnp.int32, (nq, CHUNK), 1)
        values = jnp.where(place < lens[r], values, NEGATIVE)
        merge(r, values, cache_v[r, c * CHUNK : (c + 1) * CHUNK, :])

    late = LATE
    for i in range(late):
        if i in FLAG_STEPS:
            flag_step(FLAG_STEPS[i])
        take(i)

    for copy in sent_p:
        copy.wait_recv()
    other = yrecv[1, 0]
    for k in range(1, zs):
        projected = projected + yrecv[0, k]
        other = other + yrecv[1, k]
    is_key = lane < half
    squares = jnp.sum(jnp.where(is_key, projected * projected, 0.0), axis=1, keepdims=True)
    squares = squares + jnp.sum(jnp.where(is_key, other * other, 0.0), axis=1, keepdims=True)
    inverse = lax.rsqrt(squares / HD + EPSILON)
    gains = jnp.broadcast_to(gain_v[...], (8, HD))
    swapped = pltpu.roll(gains, half, 1)
    own_gain = jnp.where(first, gains, swapped)
    other_gain = jnp.where(first, swapped, gains)
    entries = jnp.where(is_key, projected * inverse * own_gain, projected)
    other_keys = jnp.where(is_key, other * inverse * other_gain, 0.0)
    for s in range(steps):
        both_out[s, :, 0:HD] = entries[s * rows : (s + 1) * rows, :].astype(BF16)
    blank = jnp.zeros((8, HD), F32)
    own16 = jnp.concatenate([entries, blank], axis=0).astype(BF16)
    other16 = jnp.concatenate([other_keys, blank], axis=0).astype(BF16)
    column = lax.broadcasted_iota(jnp.int32, (nq, 16), 1)
    step_of = lax.broadcasted_iota(jnp.int32, (nq, 16), 0) // group
    for r in range(rows):
        fresh = lax.dot_general(qbf[r], own16, (((1,), (1,)), ((), ())), preferred_element_type=F32)
        fresh = fresh + lax.dot_general(qoth[r], other16, (((1,), (1,)), ((), ())), preferred_element_type=F32)
        allowed = (column % rows == r) & (column // rows <= step_of)
        merge(r, jnp.where(allowed, fresh * factor, NEGATIVE), own16)

    for i in range(late, nchunk):
        take(i)

    result = [acc[r] / den[r] for r in range(rows)]
    right = (lane >= half) == odd
    for s in range(steps):
        lines = []
        for r in range(rows):
            part = result[r][s * group : (s + 1) * group, :]
            part = jnp.where(odd, part, pltpu.roll(part, half, 1))
            part = jnp.where(right, part, 0.0)
            lines.append(
                [
                    jnp.sum(jnp.where(sub // 2 == j, part, 0.0), axis=0, keepdims=True)
                    for j in range(group * half // HD)
                ]
            )
        for j in range(group * half // HD):
            both_out[s, :, (j + 1) * HD : (j + 2) * HD] = jnp.concatenate([line[j] for line in lines], axis=0).astype(BF16)

    if not exact:

        @pl.when(first)
        def _():
            flag_out[...] = fl[3]
            for stage in range(4):
                for copy in described(stage):
                    copy.wait_send()

        @pl.when(jnp.logical_not(first))
        def _():
            described(3)[0].wait_recv()
            flag_out[...] = fp[...]

    for copy in main + [sent_q] + sent_h + sent_w + sent_p:
        copy.wait_send()


def fused(sizes, exact, hidden, base_kv, delta_codes, block_scales, key_gain, queries, kv_cache, lengths):
    zs, xcs, ys = sizes
    step_count, row_count, width = hidden.shape
    cache_length = kv_cache.shape[1]
    nq = step_count * 8
    nchunk = row_count * cache_length // CHUNK
    own_blocks = width // BLOCK // zs
    dma = pltpu.SemaphoreType.DMA
    any_space = pl.BlockSpec(memory_space=pl.ANY)
    smem = pl.BlockSpec(memory_space=pltpu.SMEM)
    vmem = pl.BlockSpec(memory_space=pltpu.VMEM)
    return pl.pallas_call(
        functools.partial(pair_kernel, zs, xcs, ys, exact),
        out_shape=(
            jax.ShapeDtypeStruct((step_count, row_count, HD + queries.shape[2]), BF16),
        )
        + (() if exact else (jax.ShapeDtypeStruct((8, HD), F32),)),
        in_specs=[any_space, any_space, any_space, smem, any_space, any_space, any_space, smem],
        out_specs=(vmem,) if exact else (vmem, vmem),
        scratch_shapes=[
            pltpu.VMEM(queries.shape, BF16),
            pltpu.VMEM(hidden.shape, BF16),
            pltpu.VMEM(base_kv.shape, BF16),
            pltpu.VMEM((1, HD), F32),
            pltpu.VMEM(kv_cache.shape, BF16),
            pltpu.VMEM((xcs,) + delta_codes.shape, BF16),
            pltpu.VMEM((row_count, nq, HD), F32),
            pltpu.VMEM((row_count, nq, HD), BF16),
            pltpu.VMEM((2, nq, HD), BF16),
            pltpu.VMEM((row_count, nq, HD), BF16),
            pltpu.VMEM((step_count * row_count, width), F32),
            pltpu.VMEM((zs, own_blocks * 8, BLOCK), BF16),
            pltpu.VMEM((zs - 1, own_blocks * 8, BLOCK), BF16),
            pltpu.VMEM((nchunk, nq, CHUNK), F32),
            pltpu.VMEM((1, nq, HD) if exact else (nchunk, nq, CHUNK), jnp.int16),
            pltpu.VMEM((nchunk, nq, CHUNK), F32 if exact else jnp.int16),
            pltpu.VMEM((zs, 8, HD), F32),
            pltpu.VMEM((2, zs, 8, HD), F32),
            pltpu.VMEM((4, 8, HD), F32),
            pltpu.VMEM((ys - 1, 8, HD), F32),
            pltpu.VMEM((xcs - 1, 8, HD), F32),
            pltpu.VMEM((zs - 1, 8, HD), F32),
            pltpu.VMEM((8, HD), F32),
            dma((5,)),
            dma((nchunk,)),
            dma((nchunk,)),
            dma((nchunk,)),
            dma,
            dma,
            dma((xcs - 1,)),
            dma((xcs - 1,)),
            dma((zs - 1,)),
            dma((zs - 1,)),
            dma((2, zs)),
            dma((2, zs)),
            dma((ys - 1,)),
            dma((ys - 1,)),
            dma((xcs - 1,)),
            dma((xcs - 1,)),
            dma((zs - 1,)),
            dma((zs - 1,)),
            dma,
            dma,
        ],
        compiler_params=pltpu.CompilerParams(
            collective_id=1 if exact else 0, has_side_effects=True
        ),
    )(hidden, base_kv, delta_codes, block_scales.T, key_gain.reshape(1, HD), queries, kv_cache, lengths)


def local(sizes, *args):
    both, widest = fused(sizes, False, *args)
    both = lax.cond(
        widest[0, 0] <= NORM_LIMIT,
        lambda args, fast: fast,
        lambda args, fast: fused(sizes, True, *args)[0],
        args,
        both,
    )
    return both[:, :, :HD], both[:, :, HD:]


def solution(mesh):
    fsdp, tp = mesh.shape["fsdp"], mesh.shape["tp"]
    sizes = (4, fsdp // 4, tp // 2)
    in_specs = (
        P(None, "fsdp", None),
        P(None, "tp"),
        P("fsdp", "tp"),
        P(None, "tp"),
        P(),
        P(None, "fsdp", "tp"),
        P("fsdp", None, "tp"),
        P("fsdp"),
    )
    out_specs = (P(None, "fsdp", "tp"), P(None, "fsdp", "tp"))
    return jax.shard_map(
        functools.partial(local, sizes), mesh=mesh, in_specs=in_specs, out_specs=out_specs, check_vma=False
    )
```

time: 206 us -> 110 us (0.53)
  waiting for transfers between devices: 65.6 us -> 0 us
  Pallas kernels: 53.1 us -> 106 us
  starting transfers between devices: 45.8 us -> 0 us
  between operations: 14.8 us -> 1.4 us
  matrix products: 11.9 us -> 0 us
  local copies, waits for them, and re-layouts: 8.73 us -> 2.41 us
  other arithmetic: 3.65 us -> 0 us
    pallas_call x1 -> x2, Pallas kernels: 53.1 us -> 106 us  [fused(): pl.pallas_call(functools.partial(pair_kernel, zs, xcs, ys, exact), out_sh...]
    ppermute x9 -> x0, starting transfers between devices: 45.8 us -> none  [partner(): return lax.ppermute(block, axis, route)]
    ppermute x9 -> x0, waiting for transfers between devices: 33 us -> none  [partner(): return lax.ppermute(block, axis, route)]
    all_gather x1 -> x0, waiting for transfers between devices: 31.9 us -> none  [plain(): lax.all_gather(delta_codes, 'fsdp', axis=0, tiled=True).astype(jnp.float32)]
    dot_general x18 -> x0, matrix products: 11.9 us -> none  [the longest x4 3.85 us: plain(): jnp.einsum('srugd,rlud->srugl', query_step, cache_keys, preferred_element...]
    another operation x5 -> x0, local copies, waits for them, and re-layouts: 3.25 us -> none
    unnamed x15 -> x12, local copies, waits for them, and re-layouts: 2.74 us -> 0.03 us
    reduce_max x5 -> x0, other arithmetic: 2.15 us -> none  [the longest x1 1.81 us: attend(): jnp.max(cache_logits, axis=-1)]
  transfers between devices with their start and end apart: 10 -> 0, of which waited for: 7 -> 0; matrix products, arithmetic and copies ran while one was open for 7% -> 0% of each run, Pallas kernels for 0% -> 0%
where the time goes in v2:
time: 110 us; the launch traced here: 109 us
  Pallas kernels  106 us (96%)
  local copies, waits for them, and re-layouts  2.41 us (2%)
  between operations  1.4 us (1%)
    pallas_call x2, Pallas kernels, fused(): pl.pallas_call(functools.partial(pair_kernel, zs, xcs, ys, exact), out_sh...  106 us

profile of v2, /device:TPU:6, one launch (start us, length us, event | category | flops | bytes accessed | tf_op | source)
XLA Modules:
  0.0 109.4 jit_solution(14575264173808318302)
XLA Ops:
  0.6 0.0 copy-start
  0.6 0.0 copy-start.4
  0.7 0.0 copy-start.5
  0.7 0.0 copy-start.3
  0.7 0.0 copy-start.1
  0.7 0.0 copy-start.2
  0.7 42.7 %shard_map.95 = (bf16[4,2,640]{2,1,0:T(2,128)(2,1)S(1)}, f32[8,128]{1,0:T(8,128)}) custom-call(bf16[4,2,5120]{2,1,0:T(2,128)(2,1)} %hid.1, bf16[5120,128]{1,0:T(8,128)(2,1)} %base.1, bf16[160,128]{1,0:T(8,128)(2,1)} %codes.1, f32[1,40]{1,0:T(1,128)} %bitcast.5, f32[1,128]{1,0:T(1,128)} %bitcast.7, bf16[4,2,512]{2,1,0:T(2,128)(2,1)} %qry.1, ...), custom_call_target="tpu_custom_call" | custom-call | tf_op jit(solution)/shard_map/pallas_call | solution.py:364
  43.4 1.2 %slice.9 = f32[1,1]{1,0:T(1,128)} slice(f32[8,128]{1,0:T(8,128)} %get-tuple-element.32), slice={[0:1], [0:1]} | slice | bytes 8 | tf_op jit(solution)/shard_map/slice | solution.py:426
  45.2 0.0 copy-done
  45.3 0.0 copy-done.4
  45.3 0.0 copy-done.5
  45.3 0.0 copy-done.3
  45.3 0.0 copy-done.1
  45.3 0.0 copy-done.2
  45.3 62.9 %conditional.1 = (bf16[4,2,640]{2,1,0:T(2,128)(2,1)S(1)}) conditional(s32[]{:T(128)} %bitcast.4, (f32[40,1]{0,1:T(1,128)S(1)}, f32[128]{0:T(128)}, bf16[4,2,5120]{2,1,0:T(2,128)(2,1)S(1)}, bf16[5120,128]{1,0:T(8,128)(2,1)S(1)}, bf16[160,128]{1,0:T(8,128)(2,1)S(1)}, /*index=5*/bf16[4,2,512]{2,1,0:T(2,128)(2,1)S(1)}, ...), branch_computations={%region_0.0_spmd, %region_1.0_spmd} | conditional | bytes 8 | solution.py:425
  45.3 62.9 %branch_0_fun.1 = bf16[4,2,640]{2,1,0:T(2,128)(2,1)S(1)} custom-call(bf16[4,2,5120]{2,1,0:T(2,128)(2,1)S(1)} %get-tuple-element.20.hid, bf16[5120,128]{1,0:T(8,128)(2,1)S(1)} %get-tuple-element.21.base, bf16[160,128]{1,0:T(8,128)(2,1)S(1)} %get-tuple-element.22.codes, f32[1,40]{1,0:T(1,128)S(1)} %bitcast.6, f32[1,128]{1,0:T(1,128)} %bitcast.8, ...), custom_call_target="tpu_custom_call" | custom-call | tf_op jit(solution)/shard_map/cond/branch_0_fun/pallas_call | solution.py:364
  108.2 0.6 slice.10
  108.8 0.6 slice.11
Async XLA Ops:
  0.6 44.6 %copy-start = (bf16[2,4096,128]{2,1,0:T(8,128)(2,1)S(1)}, bf16[2,4096,128]{2,1,0:T(8,128)(2,1)}, u32[]{:S(2)}) copy-start(bf16[2,4096,128]{2,1,0:T(8,128)(2,1)} %cache.1) | copy-start | bytes 6291460
  0.6 44.6 %copy-start.4 = (bf16[4,2,512]{2,1,0:T(2,128)(2,1)S(1)}, bf16[4,2,512]{2,1,0:T(2,128)(2,1)}, u32[]{:S(2)}) copy-start(bf16[4,2,512]{2,1,0:T(2,128)(2,1)} %qry.1) | copy-start | bytes 24580
  0.7 44.6 %copy-start.5 = (f32[40,1]{0,1:T(1,128)S(1)}, f32[40,1]{0,1:T(1,128)}, u32[]{:S(2)}) copy-start(f32[40,1]{0,1:T(1,128)} %param.13) | copy-start | bytes 484
  0.7 44.6 %copy-start.3 = (bf16[160,128]{1,0:T(8,128)(2,1)S(1)}, bf16[160,128]{1,0:T(8,128)(2,1)}, u32[]{:S(2)}) copy-start(bf16[160,128]{1,0:T(8,128)(2,1)} %codes.1) | copy-start | bytes 122884
  0.7 44.6 %copy-start.1 = (bf16[5120,128]{1,0:T(8,128)(2,1)S(1)}, bf16[5120,128]{1,0:T(8,128)(2,1)}, u32[]{:S(2)}) copy-start(bf16[5120,128]{1,0:T(8,128)(2,1)} %base.1) | copy-start | bytes 3932164
  0.7 44.6 %copy-start.2 = (bf16[4,2,5120]{2,1,0:T(2,128)(2,1)S(1)}, bf16[4,2,5120]{2,1,0:T(2,128)(2,1)}, u32[]{:S(2)}) copy-start(bf16[4,2,5120]{2,1,0:T(2,128)(2,1)} %hid.1) | copy-start | bytes 245764

commit v3 on v2

--- a/solution.py
+++ b/solution.py
@@ -23,7 +23,8 @@
 F32 = jnp.float32
 BF16 = jnp.bfloat16
 CHUNK = 1024
-LATE = 8
+LATE = 6
+EARLY = 5
 FLAG_STEPS = {2: 2, 5: 3}
 
 
@@ -72,10 +73,10 @@
 
     barrier = pltpu.get_barrier_semaphore()
     everyone = (
-        [partner]
-        + [z_peer(k) for k in range(1, zs)]
+        [z_peer(k) for k in range(1, zs)]
+        + [x_peer(k) for k in range(1, xcs)]
+        + [partner]
         + [other_z_peer(k) for k in range(1, zs)]
-        + [x_peer(k) for k in range(1, xcs)]
     )
     for device in everyone:
         pl.semaphore_signal(barrier, inc=1, device_id=device, device_id_type=MESH)
@@ -178,7 +179,13 @@
     ]
     sent_q = remote(packed.at[0], packed.at[1], qx_s, qx_r, partner)
     parts = lown if exact else snd
-    main = [remote(parts.at[i], rcv.at[i], main_s.at[i], main_r.at[i], partner) for i in range(nchunk)]
+
+    def send_main(low, high):
+        return [
+            remote(parts.at[i], rcv.at[i], main_s.at[i], main_r.at[i], partner) for i in range(low, high)
+        ]
+
+    main = send_main(0, EARLY)
 
     get_b.wait()
     get_g.wait()
@@ -254,6 +261,7 @@
         for side, device in enumerate((z_peer(zs - k), other_z_peer(zs - k))):
             sent_p.append(remote(ysend.at[k], yrecv.at[side, k], p2_s.at[side, k], p2_r.at[side, k], device))
 
+    main += send_main(EARLY, nchunk)
     flag_step(1)
 
     top = [jnp.full((nq, 1), NEGATIVE, F32) for _ in range(rows)]
@@ -336,7 +344,7 @@
 
         @pl.when(first)
         def _():
-            flag_out[...] = fl[3]
+            fp[...] = fl[3]
             for stage in range(4):
                 for copy in described(stage):
                     copy.wait_send()
@@ -344,7 +352,8 @@
         @pl.when(jnp.logical_not(first))
         def _():
             described(3)[0].wait_recv()
-            flag_out[...] = fp[...]
+
+        flag_out[0] = jnp.where(jnp.max(fp[...]) <= NORM_LIMIT, 1, 0).astype(jnp.int32)
 
     for copy in main + [sent_q] + sent_h + sent_w + sent_p:
         copy.wait_send()
@@ -366,9 +375,9 @@
         out_shape=(
             jax.ShapeDtypeStruct((step_count, row_count, HD + queries.shape[2]), BF16),
         )
-        + (() if exact else (jax.ShapeDtypeStruct((8, HD), F32),)),
+        + (() if exact else (jax.ShapeDtypeStruct((1,), jnp.int32),)),
         in_specs=[any_space, any_space, any_space, smem, any_space, any_space, any_space, smem],
-        out_specs=(vmem,) if exact else (vmem, vmem),
+        out_specs=(vmem,) if exact else (vmem, smem),
         scratch_shapes=[
             pltpu.VMEM(queries.shape, BF16),
             pltpu.VMEM(hidden.shape, BF16),
@@ -420,16 +429,27 @@
     )(hidden, base_kv, delta_codes, block_scales.T, key_gain.reshape(1, HD), queries, kv_cache, lengths)
 
 
+def split_kernel(both, new_entries, attended):
+    new_entries[...] = both[:, :, :HD]
+    attended[...] = both[:, :, HD:]
+
+
 def local(sizes, *args):
-    both, widest = fused(sizes, False, *args)
+    both, narrow = fused(sizes, False, *args)
     both = lax.cond(
-        widest[0, 0] <= NORM_LIMIT,
+        narrow[0] != 0,
         lambda args, fast: fast,
         lambda args, fast: fused(sizes, True, *args)[0],
         args,
         both,
     )
-    return both[:, :, :HD], both[:, :, HD:]
+    return pl.pallas_call(
+        split_kernel,
+        out_shape=(
+            jax.ShapeDtypeStruct(both.shape[:2] + (HD,), BF16),
+            jax.ShapeDtypeStruct(both.shape[:2] + (both.shape[2] - HD,), BF16),
+        ),
+    )(both)
 
 
 def solution(mesh):

time: 110 us -> 110 us (level)
  the two profiles are of different devices: /device:TPU:6 before, /device:TPU:88 now
where the time goes in v3:
time: 110 us
  Pallas kernels  109 us (99%)
  between operations  1.42 us (1%)
    pallas_call x2, Pallas kernels, fused(): pl.pallas_call(functools.partial(pair_kernel, zs, xcs, ys, exact), out_sh...  108 us

profile of v3, /device:TPU:88, one launch (start us, length us, event | category | flops | bytes accessed | tf_op | source)
XLA Modules:
  0.0 110.2 jit_solution(5222997516162882351)
XLA Ops:
  0.6 0.0 copy-start
  0.6 0.0 copy-start.4
  0.7 0.0 copy-start.5
  0.7 0.0 copy-start.3
  0.7 0.0 copy-start.1
  0.7 0.0 copy-start.2
  0.7 41.7 %shard_map.95 = (bf16[4,2,640]{2,1,0:T(2,128)(2,1)S(1)}, s32[1]{0:T(128)}) custom-call(bf16[4,2,5120]{2,1,0:T(2,128)(2,1)} %hid.1, bf16[5120,128]{1,0:T(8,128)(2,1)} %base.1, bf16[160,128]{1,0:T(8,128)(2,1)} %codes.1, f32[1,40]{1,0:T(1,128)} %bitcast.5, f32[1,128]{1,0:T(1,128)} %bitcast.7, bf16[4,2,512]{2,1,0:T(2,128)(2,1)} %qry.1, ...), custom_call_target="tpu_custom_call" | custom-call | tf_op jit(solution)/shard_map/pallas_call | solution.py:373
  43.1 0.0 copy-done
  43.1 0.0 copy-done.4
  43.1 0.0 copy-done.5
  43.1 0.0 copy-done.3
  43.1 0.0 copy-done.1
  43.2 0.0 copy-done.2
  43.2 66.5 %conditional.1 = (bf16[4,2,640]{2,1,0:T(2,128)(2,1)S(1)}) conditional(s32[]{:T(128)} %bitcast.4, (f32[40,1]{0,1:T(1,128)S(1)}, f32[128]{0:T(128)}, bf16[4,2,5120]{2,1,0:T(2,128)(2,1)S(1)}, bf16[5120,128]{1,0:T(8,128)(2,1)S(1)}, bf16[160,128]{1,0:T(8,128)(2,1)S(1)}, /*index=5*/bf16[4,2,512]{2,1,0:T(2,128)(2,1)S(1)}, ...), branch_computations={%region_0.0_spmd, %region_1.0_spmd} | conditional | bytes 8 | solution.py:439
  43.2 66.4 %branch_0_fun.1 = bf16[4,2,640]{2,1,0:T(2,128)(2,1)S(1)} custom-call(bf16[4,2,5120]{2,1,0:T(2,128)(2,1)S(1)} %get-tuple-element.20.hid, bf16[5120,128]{1,0:T(8,128)(2,1)S(1)} %get-tuple-element.21.base, bf16[160,128]{1,0:T(8,128)(2,1)S(1)} %get-tuple-element.22.codes, f32[1,40]{1,0:T(1,128)S(1)} %bitcast.6, f32[1,128]{1,0:T(1,128)} %bitcast.8, ...), custom_call_target="tpu_custom_call" | custom-call | tf_op jit(solution)/shard_map/cond/branch_0_fun/pallas_call | solution.py:373
  109.6 0.6 shard_map.96
Async XLA Ops:
  0.6 42.5 %copy-start = (bf16[2,4096,128]{2,1,0:T(8,128)(2,1)S(1)}, bf16[2,4096,128]{2,1,0:T(8,128)(2,1)}, u32[]{:S(2)}) copy-start(bf16[2,4096,128]{2,1,0:T(8,128)(2,1)} %cache.1) | copy-start | bytes 6291460
  0.6 42.5 %copy-start.4 = (bf16[4,2,512]{2,1,0:T(2,128)(2,1)S(1)}, bf16[4,2,512]{2,1,0:T(2,128)(2,1)}, u32[]{:S(2)}) copy-start(bf16[4,2,512]{2,1,0:T(2,128)(2,1)} %qry.1) | copy-start | bytes 24580
  0.7 42.5 %copy-start.5 = (f32[40,1]{0,1:T(1,128)S(1)}, f32[40,1]{0,1:T(1,128)}, u32[]{:S(2)}) copy-start(f32[40,1]{0,1:T(1,128)} %param.13) | copy-start | bytes 484
  0.7 42.5 %copy-start.3 = (bf16[160,128]{1,0:T(8,128)(2,1)S(1)}, bf16[160,128]{1,0:T(8,128)(2,1)}, u32[]{:S(2)}) copy-start(bf16[160,128]{1,0:T(8,128)(2,1)} %codes.1) | copy-start | bytes 122884
  0.7 42.5 %copy-start.1 = (bf16[5120,128]{1,0:T(8,128)(2,1)S(1)}, bf16[5120,128]{1,0:T(8,128)(2,1)}, u32[]{:S(2)}) copy-start(bf16[5120,128]{1,0:T(8,128)(2,1)} %base.1) | copy-start | bytes 3932164
  0.7 42.5 %copy-start.2 = (bf16[4,2,5120]{2,1,0:T(2,128)(2,1)S(1)}, bf16[4,2,5120]{2,1,0:T(2,128)(2,1)}, u32[]{:S(2)}) copy-start(bf16[4,2,5120]{2,1,0:T(2,128)(2,1)} %hid.1) | copy-start | bytes 245764

commit v4 on v3

--- a/solution.py
+++ b/solution.py
@@ -23,9 +23,9 @@
 F32 = jnp.float32
 BF16 = jnp.bfloat16
 CHUNK = 1024
-LATE = 6
+LATE = 8
 EARLY = 5
-FLAG_STEPS = {2: 2, 5: 3}
+FLAG_STEPS = {2: 2, 7: 3}
 
 
 def pair_kernel(

time: 110 us -> 109 us (level)
  the two profiles are of different devices: /device:TPU:88 before, /device:TPU:206 now
where the time goes in v4:
time: 109 us
  Pallas kernels  107 us (98%)
  between operations  1.42 us (1%)
    pallas_call x2, Pallas kernels, fused(): pl.pallas_call(functools.partial(pair_kernel, zs, xcs, ys, exact), out_sh...  107 us

profile of v4, /device:TPU:206, one launch (start us, length us, event | category | flops | bytes accessed | tf_op | source)
XLA Modules:
  0.0 108.7 jit_solution(320277830849567710)
XLA Ops:
  0.6 0.0 copy-start
  0.6 0.0 copy-start.4
  0.7 0.0 copy-start.5
  0.7 0.0 copy-start.3
  0.7 0.0 copy-start.1
  0.7 0.0 copy-start.2
  0.7 38.5 %shard_map.95 = (bf16[4,2,640]{2,1,0:T(2,128)(2,1)S(1)}, s32[1]{0:T(128)}) custom-call(bf16[4,2,5120]{2,1,0:T(2,128)(2,1)} %hid.1, bf16[5120,128]{1,0:T(8,128)(2,1)} %base.1, bf16[160,128]{1,0:T(8,128)(2,1)} %codes.1, f32[1,40]{1,0:T(1,128)} %bitcast.5, f32[1,128]{1,0:T(1,128)} %bitcast.7, bf16[4,2,512]{2,1,0:T(2,128)(2,1)} %qry.1, ...), custom_call_target="tpu_custom_call" | custom-call | tf_op jit(solution)/shard_map/pallas_call | solution.py:373
  39.9 0.0 copy-done
  39.9 0.0 copy-done.4
  39.9 0.0 copy-done.5
  39.9 0.0 copy-done.3
  39.9 0.0 copy-done.1
  40.0 0.0 copy-done.2
  40.0 68.2 %conditional.1 = (bf16[4,2,640]{2,1,0:T(2,128)(2,1)S(1)}) conditional(s32[]{:T(128)} %bitcast.4, (f32[40,1]{0,1:T(1,128)S(1)}, f32[128]{0:T(128)}, bf16[4,2,5120]{2,1,0:T(2,128)(2,1)S(1)}, bf16[5120,128]{1,0:T(8,128)(2,1)S(1)}, bf16[160,128]{1,0:T(8,128)(2,1)S(1)}, /*index=5*/bf16[4,2,512]{2,1,0:T(2,128)(2,1)S(1)}, ...), branch_computations={%region_0.0_spmd, %region_1.0_spmd} | conditional | bytes 8 | solution.py:439
  40.0 68.1 %branch_0_fun.1 = bf16[4,2,640]{2,1,0:T(2,128)(2,1)S(1)} custom-call(bf16[4,2,5120]{2,1,0:T(2,128)(2,1)S(1)} %get-tuple-element.20.hid, bf16[5120,128]{1,0:T(8,128)(2,1)S(1)} %get-tuple-element.21.base, bf16[160,128]{1,0:T(8,128)(2,1)S(1)} %get-tuple-element.22.codes, f32[1,40]{1,0:T(1,128)S(1)} %bitcast.6, f32[1,128]{1,0:T(1,128)} %bitcast.8, ...), custom_call_target="tpu_custom_call" | custom-call | tf_op jit(solution)/shard_map/cond/branch_0_fun/pallas_call | solution.py:373
  108.1 0.6 shard_map.96
Async XLA Ops:
  0.6 39.3 %copy-start = (bf16[2,4096,128]{2,1,0:T(8,128)(2,1)S(1)}, bf16[2,4096,128]{2,1,0:T(8,128)(2,1)}, u32[]{:S(2)}) copy-start(bf16[2,4096,128]{2,1,0:T(8,128)(2,1)} %cache.1) | copy-start | bytes 6291460
  0.6 39.3 %copy-start.4 = (bf16[4,2,512]{2,1,0:T(2,128)(2,1)S(1)}, bf16[4,2,512]{2,1,0:T(2,128)(2,1)}, u32[]{:S(2)}) copy-start(bf16[4,2,512]{2,1,0:T(2,128)(2,1)} %qry.1) | copy-start | bytes 24580
  0.7 39.3 %copy-start.5 = (f32[40,1]{0,1:T(1,128)S(1)}, f32[40,1]{0,1:T(1,128)}, u32[]{:S(2)}) copy-start(f32[40,1]{0,1:T(1,128)} %param.13) | copy-start | bytes 484
  0.7 39.3 %copy-start.3 = (bf16[160,128]{1,0:T(8,128)(2,1)S(1)}, bf16[160,128]{1,0:T(8,128)(2,1)}, u32[]{:S(2)}) copy-start(bf16[160,128]{1,0:T(8,128)(2,1)} %codes.1) | copy-start | bytes 122884
  0.7 39.3 %copy-start.1 = (bf16[5120,128]{1,0:T(8,128)(2,1)S(1)}, bf16[5120,128]{1,0:T(8,128)(2,1)}, u32[]{:S(2)}) copy-start(bf16[5120,128]{1,0:T(8,128)(2,1)} %base.1) | copy-start | bytes 3932164
  0.7 39.3 %copy-start.2 = (bf16[4,2,5120]{2,1,0:T(2,128)(2,1)S(1)}, bf16[4,2,5120]{2,1,0:T(2,128)(2,1)}, u32[]{:S(2)}) copy-start(bf16[4,2,5120]{2,1,0:T(2,128)(2,1)} %hid.1) | copy-start | bytes 245764
